TPU v7x, 256 devices: a whole 4x4x8 slice. The times are simulated.
256 devices in a mesh: dp: 8 (over y, core), ctx: 32 (over z, x).
Axes of the slice: x: 4, y: 4, z: 8, core: 2. Of those that a mesh axis runs over, the one named last changes fastest.
Arguments:
- attention_query_rows: bfloat16 [32768, 2560], P(('dp', 'ctx')), parts along dimension 0, may hold values from -24 to 24
- key_rows: bfloat16 [32768, 512], P(('dp', 'ctx')), parts along dimension 0, may hold values from -24 to 24
- attention_value_rows: bfloat16 [32768, 512], P(('dp', 'ctx')), parts along dimension 0, may hold values from -6 to 6
- out_grad: bfloat16 [32768, 2560], P(('dp', 'ctx')), parts along dimension 0, may hold values from -6 to 6
- subset_sizes: int32 [128], P('dp'), parts along dimension 0, may hold values from 1 to 4, 32 in all
- ffn_order: int32 [256, 128], P(('dp', 'ctx')), parts along dimension 0, may hold values from 0 to 127, each once within a row
- attn_order: int32 [256, 128], P(('dp', 'ctx')), parts along dimension 0, may hold values from 0 to 127, each once within a row
Outputs:
- attn_out: bfloat16 [32768, 2560], P(('dp', 'ctx')), parts along dimension 0
- query_grad: bfloat16 [32768, 2560], P(('dp', 'ctx')), parts along dimension 0
- key_grad: bfloat16 [32768, 512], P(('dp', 'ctx')), parts along dimension 0
- value_grad: bfloat16 [32768, 512], P(('dp', 'ctx')), parts along dimension 0
There are 8 independent parts, one for each index of `dp`. A program takes and returns all parts, laid end to end along the dimension named above; each array names one. Nothing has to cross between parts.
Inputs may be any that keep to these rules, and one draw needn't show every extreme that they name: `subset_sizes`: they sum to 32, and the largest equals 4. `ffn_order`: each row holds every number once. `attn_order`: each row holds every number once.
All inputs are finite; a program needn't handle non-finite values.
Results may differ from a plain program's by a relative error of at most 0.028.
Values may be sent and summed in bfloat16 or wider, within the bound.
A program may use at most 64 MiB of HBM per device.

v0:
```python
import functools
import math

import jax
import jax.numpy as jnp
from jax import lax
from jax.sharding import PartitionSpec as P

HEAD_SIZE = 128
SUB = 4


def from_behind(x, axis, by):
    devices = lax.axis_size(axis)
    pairs = [(i, i + by) for i in range(devices) if 0 <= i + by < devices]
    return lax.ppermute(x, axis, pairs)


def device_meta(subset_sizes, device, device_count):
    end_points = jnp.cumsum(subset_sizes)
    trace_count = subset_sizes.shape[0]
    trace_id = jnp.sum((end_points[None, :] <= device[:, None]).astype(jnp.int32), axis=1)
    one_hot = (jnp.arange(trace_count, dtype=jnp.int32)[None, :] == trace_id[:, None]).astype(
        jnp.int32
    )
    span_size = jnp.sum(one_hot * subset_sizes[None, :], axis=1)
    first_device = jnp.sum(one_hot * (end_points - subset_sizes)[None, :], axis=1)
    in_range = (device >= 0) & (device < device_count)
    return (jnp.where(in_range, trace_id, -1), device - first_device, span_size)


def row_positions(member, span_size, row_count):
    half_rows = row_count // 2
    local_rows = jnp.arange(row_count, dtype=jnp.int32)[None, :]
    first_half = member[:, None] * half_rows + local_rows
    second_half = (
        (2 * span_size[:, None] - 1 - member[:, None]) * half_rows + local_rows - half_rows
    )
    return jnp.where(local_rows < half_rows, first_half, second_half)


def body(
    attention_query_rows,
    key_rows,
    attention_value_rows,
    out_grad,
    subset_sizes,
    ffn_order,
    attn_order,
):
    device_count = lax.axis_size("ctx")
    own_index = lax.axis_index("ctx")
    row_count = attention_query_rows.shape[0]
    peer_rows = row_count // device_count
    distance = SUB - 1
    key_value_width = key_rows.shape[1]
    kv_heads = key_value_width // HEAD_SIZE
    groups = attention_query_rows.shape[1] // key_value_width
    score_scale = 1.0 / math.sqrt(HEAD_SIZE)
    ffn_perm = ffn_order[0]
    att_perm = attn_order[0]
    received = lax.all_to_all(
        out_grad[ffn_perm].reshape(device_count, peer_rows, out_grad.shape[1]),
        "ctx",
        split_axis=0,
        concat_axis=0,
        tiled=True,
    )
    flat_rows = received.reshape(row_count, received.shape[2])
    attention_gradient = jnp.zeros_like(flat_rows).at[att_perm].set(flat_rows)
    offsets = (
        [0]
        + [hop_index + 1 for hop_index in range(distance)]
        + [-(hop_index + 1) for hop_index in range(distance)]
    )
    own_pair = jnp.concatenate([key_rows, attention_value_rows], axis=1)
    pieces = {0: own_pair}
    for offset in offsets[1:]:
        pieces[offset] = from_behind(own_pair, "ctx", offset)
    piece_devices = own_index - jnp.array(offsets, dtype=jnp.int32)
    trace_ids, members, spans = device_meta(subset_sizes, piece_devices, device_count)
    positions = row_positions(members, spans, row_count)
    query_trace = trace_ids[0]
    query_pos = positions[0]
    heads_of_query = attention_query_rows.reshape(row_count, kv_heads, groups, HEAD_SIZE)
    score_list = []
    for piece_index, offset in enumerate(offsets):
        heads_of_key = pieces[offset][:, :key_value_width].reshape(row_count, kv_heads, HEAD_SIZE)
        raw_scores = (
            jnp.einsum(
                "qhgd,khd->hgqk", heads_of_query, heads_of_key, preferred_element_type=jnp.float32
            )
            * score_scale
        )
        allowed = (
            (trace_ids[piece_index] == query_trace)
            & (trace_ids[piece_index] >= 0)
            & (positions[piece_index][None, :] <= query_pos[:, None])
        )
        score_list.append(jnp.where(allowed[None, None], raw_scores, -jnp.inf))
    row_top = functools.reduce(
        jnp.maximum, [jnp.max(block, axis=-1, keepdims=True) for block in score_list]
    )
    row_total = functools.reduce(
        jnp.add, [jnp.sum(jnp.exp(block - row_top), axis=-1, keepdims=True) for block in score_list]
    )
    prob_list = [jnp.exp(block - row_top) / row_total for block in score_list]
    mixed = jnp.zeros((row_count, kv_heads, groups, HEAD_SIZE), jnp.float32)
    for piece_index, offset in enumerate(offsets):
        heads_of_value = pieces[offset][:, key_value_width:].reshape(row_count, kv_heads, HEAD_SIZE)
        prob_b = prob_list[piece_index].astype(jnp.bfloat16)
        mixed = mixed + jnp.einsum(
            "hgqk,khd->qhgd", prob_b, heads_of_value, preferred_element_type=jnp.float32
        )
    attention_apply = mixed.reshape(row_count, kv_heads * groups * HEAD_SIZE).astype(jnp.bfloat16)
    received = lax.all_to_all(
        attention_apply[att_perm].reshape(device_count, peer_rows, attention_apply.shape[1]),
        "ctx",
        split_axis=0,
        concat_axis=0,
        tiled=True,
    )
    flat_rows = received.reshape(row_count, received.shape[2])
    attn_out = jnp.zeros_like(flat_rows).at[ffn_perm].set(flat_rows)
    head_gradient = attention_gradient.reshape(row_count, kv_heads, groups, HEAD_SIZE)
    output_heads = attention_apply.reshape(row_count, kv_heads, groups, HEAD_SIZE)
    delta = jnp.einsum(
        "qhgd,qhgd->hgq", head_gradient, output_heads, preferred_element_type=jnp.float32
    )[..., None]
    query_sum = jnp.zeros((row_count, kv_heads, groups, HEAD_SIZE), jnp.float32)
    terms = {}
    for piece_index, offset in enumerate(offsets):
        heads_of_key = pieces[offset][:, :key_value_width].reshape(row_count, kv_heads, HEAD_SIZE)
        heads_of_value = pieces[offset][:, key_value_width:].reshape(row_count, kv_heads, HEAD_SIZE)
        prob = prob_list[piece_index]
        prob_b = prob.astype(jnp.bfloat16)
        dprob = jnp.einsum(
            "qhgd,khd->hgqk", head_gradient, heads_of_value, preferred_element_type=jnp.float32
        )
        dscore = (prob * (dprob - delta)).astype(jnp.bfloat16)
        query_sum = query_sum + jnp.einsum(
            "hgqk,khd->qhgd", dscore, heads_of_key, preferred_element_type=jnp.float32
        )
        key_part = (
            jnp.einsum("hgqk,qhgd->khd", dscore, heads_of_query, preferred_element_type=jnp.float32)
            * score_scale
        )
        value_part = jnp.einsum(
            "hgqk,qhgd->khd", prob_b, head_gradient, preferred_element_type=jnp.float32
        )
        terms[offset] = jnp.concatenate(
            [
                key_part.reshape(row_count, key_value_width),
                value_part.reshape(row_count, key_value_width),
            ],
            axis=1,
        ).astype(jnp.bfloat16)
    query_grad = (
        (query_sum * score_scale)
        .reshape(row_count, kv_heads * groups * HEAD_SIZE)
        .astype(jnp.bfloat16)
    )
    grad_total = terms[0].astype(jnp.float32)
    for offset in offsets[1:]:
        grad_total = grad_total + from_behind(terms[offset], "ctx", -offset).astype(jnp.float32)
    key_grad = grad_total[:, :key_value_width].astype(jnp.bfloat16)
    value_grad = grad_total[:, key_value_width:].astype(jnp.bfloat16)
    return (attn_out, query_grad, key_grad, value_grad)


def solution(mesh):
    in_specs = (
        P(("dp", "ctx"), None),
        P(("dp", "ctx"), None),
        P(("dp", "ctx"), None),
        P(("dp", "ctx"), None),
        P("dp"),
        P(("dp", "ctx"), None),
        P(("dp", "ctx"), None),
    )
    out_specs = (
        P(("dp", "ctx"), None),
        P(("dp", "ctx"), None),
        P(("dp", "ctx"), None),
        P(("dp", "ctx"), None),
    )
    return jax.shard_map(body, mesh=mesh, in_specs=in_specs, out_specs=out_specs, check_vma=False)
```

profile of v0, /device:TPU:2, one launch (start us, length us, event | category | flops | bytes accessed | tf_op | source)
XLA Modules:
  0.0 199.0 jit_solution(18051271034485492762)
XLA Ops:
  6.1 4.2 %collective-permute-start.3 = (bf16[128,1024]{0,1:T(8,128)(2,1)}, bf16[128,1024]{0,1:T(8,128)(2,1)}, u32[]{:S(2)}, u32[]{:S(2)}) collective-permute-start(bf16[128,1024]{0,1:T(8,128)(2,1)} %pad_maximum_fusion), channel_id=1, source_target_pairs={{1,0},{2,1},{3,2},{4,3},{5,4},{6,5},{7,6},{8,7},{9,8},{10,9},{11,1... | collective-permute-start | bytes 786440 | tf_op jit(solution)/shard_map/ppermute | solution.py:16
  10.3 7.3 %collective-permute-start.2 = (bf16[128,1024]{0,1:T(8,128)(2,1)}, bf16[128,1024]{0,1:T(8,128)(2,1)S(1)}, u32[]{:S(2)}, u32[]{:S(2)}) collective-permute-start(bf16[128,1024]{0,1:T(8,128)(2,1)} %pad_maximum_fusion), channel_id=1, source_target_pairs={{0,3},{1,4},{2,5},{3,6},{4,7},{5,8},{6,9},{7,10},{8,11},{9,12},{10... | collective-permute-start | bytes 786440 | tf_op jit(solution)/shard_map/ppermute | solution.py:16
  17.6 4.9 %collective-permute-start.1 = (bf16[128,1024]{0,1:T(8,128)(2,1)}, bf16[128,1024]{0,1:T(8,128)(2,1)}, u32[]{:S(2)}, u32[]{:S(2)}) collective-permute-start(bf16[128,1024]{0,1:T(8,128)(2,1)} %pad_maximum_fusion), channel_id=1, source_target_pairs={{0,2},{1,3},{2,4},{3,5},{4,6},{5,7},{6,8},{7,9},{8,10},{9,11},{10,... | collective-permute-start | bytes 786440 | tf_op jit(solution)/shard_map/ppermute | solution.py:16
  25.2 11.3 %all-to-all-start.1 = ((bf16[32,4,2560]{2,1,0:T(4,128)(2,1)}), bf16[32,4,2560]{2,1,0:T(4,128)(2,1)S(1)}, u32[]{:S(2)}, u32[]{:S(2)}) async-start(bf16[32,4,2560]{2,1,0:T(4,128)(2,1)} %reshape.547), calls=%async_computation.1 | async-start | bytes 1310720 | tf_op jit(solution)/shard_map/all_to_all | solution.py:62
  52.2 3.4 %collective-permute-start = (bf16[128,1024]{0,1:T(8,128)(2,1)}, bf16[128,1024]{0,1:T(8,128)(2,1)S(1)}, u32[]{:S(2)}, u32[]{:S(2)}) collective-permute-start(bf16[128,1024]{0,1:T(8,128)(2,1)} %pad_maximum_fusion), channel_id=1, source_target_pairs={{0,1},{1,2},{2,3},{3,4},{4,5},{5,6},{6,7},{7,8},{8,9},{9,10},{10,1... | collective-permute-start | bytes 786440 | tf_op jit(solution)/shard_map/ppermute | solution.py:16
  57.0 1.3 fusion.120
  58.7 1.3 fusion.119
  64.6 2.7 %fusion.61 = (f32[4,5,128]{2,1,0:T(8,128)S(1)}, f32[4,5,128]{2,1,0:T(8,128)S(1)}, f32[4,5,128]{2,1,0:T(8,128)S(1)}, f32[4,5,128]{2,1,0:T(8,128)S(1)}, f32[4,5,12...) fusion(f32[4,5,128,128]{2,3,1,0:T(8,128)S(1)} %get-tuple-element.76, ...), kind=kLoop, calls=%fused_computation.115 | loop fusion | flops 4569600 | bytes 9256960 | tf_op jit(solution)/shard_map/reduce_sum | solution.py:105
  67.8 1.5 convolution_bitcast_fusion.17
  69.2 1.5 convolution_bitcast_fusion.16
  70.7 1.6 convolution_bitcast_fusion.15
  72.7 1.5 fusion.39
  75.2 2.4 %scatter_custom_fusion.1 = bf16[128,2560]{1,0:T(8,128)(2,1)S(1)} fusion(s32[128]{0:T(128)} %copy-done.54, bf16[128,2560]{1,0:T(8,128)(2,1)} %reshape.592, bf16[]{:T(256)} %constant.16.clone.1), kind=kCustom, calls=%fused_computation.148 | custom fusion | bytes 655872 | tf_op jit(solution)/shard_map/scatter | solution.py:70
  78.7 2.7 %fusion.73 = bf16[4,128,128]{2,1,0:T(8,128)(2,1)} fusion(bf16[128,4,5,128]{0,3,2,1:T(8,128)(2,1)} %bitcast.492, f32[4,5,128]{2,1,0:T(8,128)} %copy-done.50, f32[4,5,128,128]{2,3,1,0:T(8,128)} %copy-done.13, f32[4,5,128]{2,1,0:T(8,128)S(1)} %maximum_maximum_fusion), kind=kOutput, calls=%fused_computation.127 | convolution fusion | flops 84934656 | bytes 2117632 | tf_op jit(solution)/shard_map/hgqk,qhgd->khd/dot_general | solution.py:148
  84.0 1.5 fusion.50
  96.3 1.3 fusion.48
  101.5 1.4 convolution_bitcast_fusion.7
  104.0 1.4 convolution_bitcast_fusion.5
  106.4 2.1 %fusion.84 = bf16[4,128,128]{1,2,0:T(8,128)(2,1)} fusion(bf16[4,5,128,128]{2,3,1,0:T(8,128)(2,1)} %fusion.42, bf16[128,4,5,128]{0,3,2,1:T(8,128)(2,1)S(1)} %bitcast.486), kind=kOutput, calls=%fused_computation.138 | convolution fusion | flops 84017152 | bytes 1441792 | tf_op jit(solution)/shard_map/hgqk,qhgd->khd/dot_general | solution.py:145
  108.5 1.7 copy.245
  110.2 1.7 pad_maximum_fusion.1
  111.8 2.5 %collective-permute-start.6 = (bf16[128,1024]{1,0:T(8,128)(2,1)}, bf16[128,1024]{1,0:T(8,128)(2,1)}, u32[]{:S(2)}, u32[]{:S(2)}) collective-permute-start(bf16[128,1024]{1,0:T(8,128)(2,1)} %pad_maximum_fusion.1), channel_id=1, source_target_pairs={{1,0},{2,1},{3,2},{4,3},{5,4},{6,5},{7,6},{8,7},{9,8},{10,9},{11,1... | collective-permute-start | bytes 786440 | tf_op jit(solution)/shard_map/ppermute | solution.py:16
  115.3 2.1 %fusion.83 = bf16[4,128,128]{1,2,0:T(8,128)(2,1)} fusion(bf16[4,5,128,128]{2,3,1,0:T(8,128)(2,1)} %fusion.43, bf16[128,4,5,128]{0,3,2,1:T(8,128)(2,1)S(1)} %bitcast.487), kind=kOutput, calls=%fused_computation.137 | convolution fusion | flops 84017152 | bytes 1441792 | tf_op jit(solution)/shard_map/hgqk,qhgd->khd/dot_general | solution.py:145
  117.4 1.7 copy.249
  119.1 1.6 pad_maximum_fusion.2
  124.1 1.6 copy.253
  125.7 1.7 pad_maximum_fusion.3
  129.7 1.7 copy.257
  131.3 1.6 pad_maximum_fusion.4
  133.0 4.0 %collective-permute-start.9 = (bf16[128,1024]{1,0:T(8,128)(2,1)}, bf16[128,1024]{1,0:T(8,128)(2,1)}, u32[]{:S(2)}, u32[]{:S(2)}) collective-permute-start(bf16[128,1024]{1,0:T(8,128)(2,1)} %pad_maximum_fusion.4), channel_id=1, source_target_pairs={{0,1},{1,2},{2,3},{3,4},{4,5},{5,6},{6,7},{7,8},{8,9},{9,10},{10,1... | collective-permute-start | bytes 786440 | tf_op jit(solution)/shard_map/ppermute | solution.py:16
  138.0 1.7 copy.261
  139.6 1.6 pad_maximum_fusion.5
  141.3 8.4 %collective-permute-start.10 = (bf16[128,1024]{1,0:T(8,128)(2,1)}, bf16[128,1024]{1,0:T(8,128)(2,1)}, u32[]{:S(2)}, u32[]{:S(2)}) collective-permute-start(bf16[128,1024]{1,0:T(8,128)(2,1)} %pad_maximum_fusion.5), channel_id=1, source_target_pairs={{0,2},{1,3},{2,4},{3,5},{4,6},{5,7},{6,8},{7,9},{8,10},{9,11},{10,... | collective-permute-start | bytes 786440 | tf_op jit(solution)/shard_map/ppermute | solution.py:16
  149.7 1.7 copy.266
  151.3 2.1 %fusion.79 = bf16[4,128,128]{1,2,0:T(8,128)(2,1)} fusion(bf16[4,5,128,128]{2,3,1,0:T(8,128)(2,1)} %fusion.48, bf16[128,4,5,128]{0,3,2,1:T(8,128)(2,1)S(1)} %bitcast.489), kind=kOutput, calls=%fused_computation.133 | convolution fusion | flops 84017152 | bytes 1441792 | tf_op jit(solution)/shard_map/hgqk,qhgd->khd/dot_general | solution.py:145
  153.4 1.7 copy.265
  155.1 1.7 copy.242
  157.5 1.5 fusion.32
  159.4 1.3 copy.214
  160.8 1.9 gather_fusion
  162.7 2.3 %reshape.545 = bf16[32,4,2560]{2,1,0:T(4,128)(2,1)} reshape(bf16[128,2560]{1,0:T(8,128)(2,1)} %gather_fusion) | data formatting | bytes 1310720 | tf_op jit(solution)/shard_map/reshape | solution.py:117
  165.0 11.2 %all-to-all-start = ((bf16[32,4,2560]{2,1,0:T(4,128)(2,1)}), bf16[32,4,2560]{2,1,0:T(4,128)(2,1)}, u32[]{:S(2)}, u32[]{:S(2)}) async-start(bf16[32,4,2560]{2,1,0:T(4,128)(2,1)} %reshape.545), calls=%async_computation | async-start | bytes 1310720 | tf_op jit(solution)/shard_map/all_to_all | solution.py:116
  176.3 1.9 pad_maximum_fusion.6
  178.5 4.1 %collective-permute-start.11 = (bf16[128,1024]{1,0:T(8,128)(2,1)}, bf16[128,1024]{1,0:T(8,128)(2,1)}, u32[]{:S(2)}, u32[]{:S(2)}) collective-permute-start(bf16[128,1024]{1,0:T(8,128)(2,1)} %pad_maximum_fusion.6), channel_id=1, source_target_pairs={{0,3},{1,4},{2,5},{3,6},{4,7},{5,8},{6,9},{7,10},{8,11},{9,12},{10... | collective-permute-start | bytes 786440 | tf_op jit(solution)/shard_map/ppermute | solution.py:16
  184.3 7.9 %collective-permute-done.11 = bf16[128,1024]{1,0:T(8,128)(2,1)} collective-permute-done((bf16[128,1024]{1,0:T(8,128)(2,1)}, bf16[128,1024]{1,0:T(8,128)(2,1)}, u32[]{:S(2)}, u32[]{:S(2)}) %collective-permute-start.11) | collective-permute-done | bytes 262176 | tf_op jit(solution)/shard_map/ppermute | solution.py:16
  192.2 1.6 add_convert_fusion
  195.1 1.5 reshape.584
  196.5 2.5 %scatter_custom_fusion = bf16[128,2560]{1,0:T(8,128)(2,1)} fusion(s32[128]{0:T(128)} %copy-done.53, bf16[128,2560]{1,0:T(8,128)(2,1)S(1)} %reshape.584, bf16[]{:T(256)} %constant.16.clone.1), kind=kCustom, calls=%fused_computation.150 | custom fusion | bytes 655872 | tf_op jit(solution)/shard_map/scatter | solution.py:124
  (202 shorter events, 52.0 us)
Async XLA Ops:
  0.6 22.5 %copy-start = (bf16[128,2560]{1,0:T(8,128)(2,1)S(1)}, bf16[128,2560]{1,0:T(8,128)(2,1)}, u32[]{:S(2)}) copy-start(bf16[128,2560]{1,0:T(8,128)(2,1)} %param.11) | copy-start | bytes 1966084
  3.5 48.7 %collective-permute-start.5 = (bf16[128,1024]{0,1:T(8,128)(2,1)}, bf16[128,1024]{0,1:T(8,128)(2,1)}, u32[]{:S(2)}, u32[]{:S(2)}) collective-permute-start(bf16[128,1024]{0,1:T(8,128)(2,1)} %pad_maximum_fusion), channel_id=1, source_target_pairs={{3,0},{4,1},{5,2},{6,3},{7,4},{8,5},{9,6},{10,7},{11,8},{12,9},{13... | collective-permute-start | bytes 786440 | tf_op jit(solution)/shard_map/ppermute | solution.py:16
  4.8 52.2 %collective-permute-start.4 = (bf16[128,1024]{0,1:T(8,128)(2,1)}, bf16[128,1024]{0,1:T(8,128)(2,1)}, u32[]{:S(2)}, u32[]{:S(2)}) collective-permute-start(bf16[128,1024]{0,1:T(8,128)(2,1)} %pad_maximum_fusion), channel_id=1, source_target_pairs={{2,0},{3,1},{4,2},{5,3},{6,4},{7,5},{8,6},{9,7},{10,8},{11,9},{12,... | collective-permute-start | bytes 786440 | tf_op jit(solution)/shard_map/ppermute | solution.py:16
  6.1 52.7 %collective-permute-start.3 = (bf16[128,1024]{0,1:T(8,128)(2,1)}, bf16[128,1024]{0,1:T(8,128)(2,1)}, u32[]{:S(2)}, u32[]{:S(2)}) collective-permute-start(bf16[128,1024]{0,1:T(8,128)(2,1)} %pad_maximum_fusion), channel_id=1, source_target_pairs={{1,0},{2,1},{3,2},{4,3},{5,4},{6,5},{7,6},{8,7},{9,8},{10,9},{11,1... | collective-permute-start | bytes 786440 | tf_op jit(solution)/shard_map/ppermute | solution.py:16
  10.3 50.2 %collective-permute-start.2 = (bf16[128,1024]{0,1:T(8,128)(2,1)}, bf16[128,1024]{0,1:T(8,128)(2,1)S(1)}, u32[]{:S(2)}, u32[]{:S(2)}) collective-permute-start(bf16[128,1024]{0,1:T(8,128)(2,1)} %pad_maximum_fusion), channel_id=1, source_target_pairs={{0,3},{1,4},{2,5},{3,6},{4,7},{5,8},{6,9},{7,10},{8,11},{9,12},{10... | collective-permute-start | bytes 786440 | tf_op jit(solution)/shard_map/ppermute | solution.py:16
  17.6 44.1 %collective-permute-start.1 = (bf16[128,1024]{0,1:T(8,128)(2,1)}, bf16[128,1024]{0,1:T(8,128)(2,1)}, u32[]{:S(2)}, u32[]{:S(2)}) collective-permute-start(bf16[128,1024]{0,1:T(8,128)(2,1)} %pad_maximum_fusion), channel_id=1, source_target_pairs={{0,2},{1,3},{2,4},{3,5},{4,6},{5,7},{6,8},{7,9},{8,10},{9,11},{10,... | collective-permute-start | bytes 786440 | tf_op jit(solution)/shard_map/ppermute | solution.py:16
  24.2 12.4 %copy-start.52 = (s32[16]{0:T(128)S(1)}, s32[16]{0:T(128)}, u32[]{:S(2)}) copy-start(s32[16]{0:T(128)} %param.12) | copy-start | bytes 196
  24.2 12.6 %copy-start.55 = (s32[7]{0:T(128)S(1)}, s32[7]{0:T(128)}, u32[]{:S(2)}) copy-start(s32[7]{0:T(128)} %constant.57) | copy-start | bytes 88
  24.2 25.5 %copy-start.35 = (bf16[128,512]{1,0:T(8,128)(2,1)S(1)}, bf16[128,512]{1,0:T(8,128)(2,1)}, u32[]{:S(2)}) copy-start(bf16[128,512]{1,0:T(8,128)(2,1)} %param.9) | copy-start | bytes 393220
  24.2 25.5 %copy-start.36 = (bf16[128,512]{1,0:T(8,128)(2,1)S(1)}, bf16[128,512]{1,0:T(8,128)(2,1)}, u32[]{:S(2)}) copy-start(bf16[128,512]{1,0:T(8,128)(2,1)} %param.10) | copy-start | bytes 393220
  24.2 26.3 %copy-start.31 = (bf16[128,2560]{1,0:T(8,128)(2,1)S(1)}, bf16[128,2560]{1,0:T(8,128)(2,1)}, u32[]{:S(2)}) copy-start(bf16[128,2560]{1,0:T(8,128)(2,1)} %param.8) | copy-start | bytes 1966084
  25.2 49.0 %all-to-all-start.1 = ((bf16[32,4,2560]{2,1,0:T(4,128)(2,1)}), bf16[32,4,2560]{2,1,0:T(4,128)(2,1)S(1)}, u32[]{:S(2)}, u32[]{:S(2)}) async-start(bf16[32,4,2560]{2,1,0:T(4,128)(2,1)} %reshape.547), calls=%async_computation.1 | async-start | bytes 1310720 | tf_op jit(solution)/shard_map/all_to_all | solution.py:62
  36.5 14.4 %copy-start.56 = (s32[1,128]{1,0:T(1,128)S(1)}, s32[1,128]{1,0:T(1,128)}, u32[]{:S(2)}) copy-start(s32[1,128]{1,0:T(1,128)} %param.14) | copy-start | bytes 1540
  51.0 5.6 %copy-start.54 = (s32[128]{0:T(128)}, s32[128]{0:T(128)S(1)}, u32[]{:S(2)}) copy-start(s32[128]{0:T(128)S(1)} %fusion.100) | copy-start | bytes 1540
  52.2 15.2 %copy-start.1 = (f32[4,5,128,128]{2,3,1,0:T(8,128)}, f32[4,5,128,128]{2,3,1,0:T(8,128)S(1)}, u32[]{:S(2)}) copy-start(f32[4,5,128,128]{2,3,1,0:T(8,128)S(1)} %get-tuple-element.74) | copy-start | bytes 3932164
  52.2 10.9 %collective-permute-start = (bf16[128,1024]{0,1:T(8,128)(2,1)}, bf16[128,1024]{0,1:T(8,128)(2,1)S(1)}, u32[]{:S(2)}, u32[]{:S(2)}) collective-permute-start(bf16[128,1024]{0,1:T(8,128)(2,1)} %pad_maximum_fusion), channel_id=1, source_target_pairs={{0,1},{1,2},{2,3},{3,4},{4,5},{5,6},{6,7},{7,8},{8,9},{9,10},{10,1... | collective-permute-start | bytes 786440 | tf_op jit(solution)/shard_map/ppermute | solution.py:16
  56.6 14.1 %copy-start.40 = (bf16[128,512]{0,1:T(8,128)(2,1)}, bf16[128,512]{0,1:T(8,128)(2,1)S(1)}, u32[]{:S(2)}) copy-start(bf16[128,512]{0,1:T(8,128)(2,1)S(1)} %get-tuple-element.38) | copy-start | bytes 393220
  57.0 13.7 %copy-start.3 = (f32[4,5,128,128]{2,3,1,0:T(8,128)}, f32[4,5,128,128]{2,3,1,0:T(8,128)S(1)}, u32[]{:S(2)}) copy-start(f32[4,5,128,128]{2,3,1,0:T(8,128)S(1)} %get-tuple-element.64) | copy-start | bytes 3932164
  58.3 10.9 %copy-start.42 = (bf16[128,512]{0,1:T(8,128)(2,1)}, bf16[128,512]{0,1:T(8,128)(2,1)S(1)}, u32[]{:S(2)}) copy-start(bf16[128,512]{0,1:T(8,128)(2,1)S(1)} %get-tuple-element.35) | copy-start | bytes 393220
  58.7 10.5 %copy-start.5 = (f32[4,5,128,128]{2,3,1,0:T(8,128)}, f32[4,5,128,128]{2,3,1,0:T(8,128)S(1)}, u32[]{:S(2)}) copy-start(f32[4,5,128,128]{2,3,1,0:T(8,128)S(1)} %get-tuple-element.66) | copy-start | bytes 3932164
  60.1 7.7 %copy-start.44 = (bf16[128,512]{0,1:T(8,128)(2,1)}, bf16[128,512]{0,1:T(8,128)(2,1)S(1)}, u32[]{:S(2)}) copy-start(bf16[128,512]{0,1:T(8,128)(2,1)S(1)} %get-tuple-element.33) | copy-start | bytes 393220
  60.5 7.3 %copy-start.7 = (f32[4,5,128,128]{2,3,1,0:T(8,128)}, f32[4,5,128,128]{2,3,1,0:T(8,128)S(1)}, u32[]{:S(2)}) copy-start(f32[4,5,128,128]{2,3,1,0:T(8,128)S(1)} %get-tuple-element.68) | copy-start | bytes 3932164
  62.7 10.0 %copy-start.46 = (bf16[128,512]{0,1:T(8,128)(2,1)}, bf16[128,512]{0,1:T(8,128)(2,1)S(1)}, u32[]{:S(2)}) copy-start(bf16[128,512]{0,1:T(8,128)(2,1)S(1)} %get-tuple-element.29) | copy-start | bytes 393220
  63.1 9.6 %copy-start.11 = (f32[4,5,128,128]{2,3,1,0:T(8,128)}, f32[4,5,128,128]{2,3,1,0:T(8,128)S(1)}, u32[]{:S(2)}) copy-start(f32[4,5,128,128]{2,3,1,0:T(8,128)S(1)} %get-tuple-element.72) | copy-start | bytes 3932164
  63.3 8.9 %copy-start.48 = (bf16[128,512]{0,1:T(8,128)(2,1)}, bf16[128,512]{0,1:T(8,128)(2,1)S(1)}, u32[]{:S(2)}) copy-start(bf16[128,512]{0,1:T(8,128)(2,1)S(1)} %get-tuple-element.31) | copy-start | bytes 393220
  64.6 7.6 %copy-start.13 = (f32[4,5,128,128]{2,3,1,0:T(8,128)}, f32[4,5,128,128]{2,3,1,0:T(8,128)S(1)}, u32[]{:S(2)}) copy-start(f32[4,5,128,128]{2,3,1,0:T(8,128)S(1)} %get-tuple-element.76) | copy-start | bytes 3932164
  64.6 2.7 %copy-start.38 = (bf16[128,4,128]{2,1,0:T(4,128)(2,1)S(1)}, bf16[128,4,128]{2,1,0:T(4,128)(2,1)}, u32[]{:S(2)}) copy-start(bf16[128,4,128]{2,1,0:T(4,128)(2,1)} %reshape.538) | copy-start | bytes 393220
  67.3 5.3 %copy-start.50 = (f32[4,5,128]{2,1,0:T(8,128)}, f32[4,5,128]{2,1,0:T(8,128)S(1)}, u32[]{:S(2)}) copy-start(f32[4,5,128]{2,1,0:T(8,128)S(1)} %add_add_fusion) | copy-start | bytes 30724
  78.7 2.7 %copy-start.12 = (f32[4,5,128,128]{2,3,1,0:T(8,128)S(1)}, f32[4,5,128,128]{2,3,1,0:T(8,128)}, u32[]{:S(2)}) copy-start(f32[4,5,128,128]{2,3,1,0:T(8,128)} %copy-done.11) | copy-start | bytes 3932164
  78.7 2.7 %copy-start.17 = (bf16[128,2560]{0,1:T(8,128)(2,1)S(1)}, bf16[128,2560]{0,1:T(8,128)(2,1)}, u32[]{:S(2)}) copy-start(bf16[128,2560]{0,1:T(8,128)(2,1)} %copy.215) | copy-start | bytes 1966084
  78.7 2.7 %copy-start.51 = (f32[4,5,128]{2,1,0:T(8,128)S(1)}, f32[4,5,128]{2,1,0:T(8,128)}, u32[]{:S(2)}) copy-start(f32[4,5,128]{2,1,0:T(8,128)} %copy-done.50) | copy-start | bytes 30724
  81.5 2.5 %copy-start.21 = (f32[128,4,5,128]{0,3,2,1:T(8,128)S(1)}, f32[128,4,5,128]{0,3,2,1:T(8,128)}, u32[]{:S(2)}) copy-start(f32[128,4,5,128]{0,3,2,1:T(8,128)} %fusion.39) | copy-start | bytes 3932164
  81.5 2.5 %copy-start.32 = (bf16[128,512]{0,1:T(8,128)(2,1)S(1)}, bf16[128,512]{0,1:T(8,128)(2,1)}, u32[]{:S(2)}) copy-start(bf16[128,512]{0,1:T(8,128)(2,1)} %get-tuple-element.27) | copy-start | bytes 393220
  101.5 2.4 %copy-start.25 = (bf16[128,512]{0,1:T(8,128)(2,1)S(1)}, bf16[128,512]{0,1:T(8,128)(2,1)}, u32[]{:S(2)}) copy-start(bf16[128,512]{0,1:T(8,128)(2,1)} %copy-done.24) | copy-start | bytes 393220
  111.8 66.7 %collective-permute-start.6 = (bf16[128,1024]{1,0:T(8,128)(2,1)}, bf16[128,1024]{1,0:T(8,128)(2,1)}, u32[]{:S(2)}, u32[]{:S(2)}) collective-permute-start(bf16[128,1024]{1,0:T(8,128)(2,1)} %pad_maximum_fusion.1), channel_id=1, source_target_pairs={{1,0},{2,1},{3,2},{4,3},{5,4},{6,5},{7,6},{8,7},{9,8},{10,9},{11,1... | collective-permute-start | bytes 786440 | tf_op jit(solution)/shard_map/ppermute | solution.py:16
  120.7 63.5 %collective-permute-start.7 = (bf16[128,1024]{1,0:T(8,128)(2,1)}, bf16[128,1024]{1,0:T(8,128)(2,1)}, u32[]{:S(2)}, u32[]{:S(2)}) collective-permute-start(bf16[128,1024]{1,0:T(8,128)(2,1)} %pad_maximum_fusion.2), channel_id=1, source_target_pairs={{2,0},{3,1},{4,2},{5,3},{6,4},{7,5},{8,6},{9,7},{10,8},{11,9},{12,... | collective-permute-start | bytes 786440 | tf_op jit(solution)/shard_map/ppermute | solution.py:16
  127.4 56.9 %collective-permute-start.8 = (bf16[128,1024]{1,0:T(8,128)(2,1)}, bf16[128,1024]{1,0:T(8,128)(2,1)}, u32[]{:S(2)}, u32[]{:S(2)}) collective-permute-start(bf16[128,1024]{1,0:T(8,128)(2,1)} %pad_maximum_fusion.3), channel_id=1, source_target_pairs={{3,0},{4,1},{5,2},{6,3},{7,4},{8,5},{9,6},{10,7},{11,8},{12,9},{13... | collective-permute-start | bytes 786440 | tf_op jit(solution)/shard_map/ppermute | solution.py:16
  133.0 51.3 %collective-permute-start.9 = (bf16[128,1024]{1,0:T(8,128)(2,1)}, bf16[128,1024]{1,0:T(8,128)(2,1)}, u32[]{:S(2)}, u32[]{:S(2)}) collective-permute-start(bf16[128,1024]{1,0:T(8,128)(2,1)} %pad_maximum_fusion.4), channel_id=1, source_target_pairs={{0,1},{1,2},{2,3},{3,4},{4,5},{5,6},{6,7},{7,8},{8,9},{9,10},{10,1... | collective-permute-start | bytes 786440 | tf_op jit(solution)/shard_map/ppermute | solution.py:16
  141.3 15.5 %copy-start.37 = (bf16[4,128,128]{1,2,0:T(8,128)(2,1)S(1)}, bf16[4,128,128]{1,2,0:T(8,128)(2,1)}, u32[]{:S(2)}) copy-start(bf16[4,128,128]{1,2,0:T(8,128)(2,1)} %fusion.85) | copy-start | bytes 393220
  141.3 43.0 %collective-permute-start.10 = (bf16[128,1024]{1,0:T(8,128)(2,1)}, bf16[128,1024]{1,0:T(8,128)(2,1)}, u32[]{:S(2)}, u32[]{:S(2)}) collective-permute-start(bf16[128,1024]{1,0:T(8,128)(2,1)} %pad_maximum_fusion.5), channel_id=1, source_target_pairs={{0,2},{1,3},{2,4},{3,5},{4,6},{5,7},{6,8},{7,9},{8,10},{9,11},{10,... | collective-permute-start | bytes 786440 | tf_op jit(solution)/shard_map/ppermute | solution.py:16
  162.7 15.5 %copy-start.15 = (bf16[4,5,128,128]{2,3,1,0:T(8,128)(2,1)S(1)}, bf16[4,5,128,128]{2,3,1,0:T(8,128)(2,1)}, u32[]{:S(2)}) copy-start(bf16[4,5,128,128]{2,3,1,0:T(8,128)(2,1)} %fusion.48) | copy-start | bytes 1966084
  165.0 17.6 %copy-start.23 = (bf16[128,512]{0,1:T(8,128)(2,1)S(1)}, bf16[128,512]{0,1:T(8,128)(2,1)}, u32[]{:S(2)}) copy-start(bf16[128,512]{0,1:T(8,128)(2,1)} %copy-done.22) | copy-start | bytes 393220
  165.0 30.0 %all-to-all-start = ((bf16[32,4,2560]{2,1,0:T(4,128)(2,1)}), bf16[32,4,2560]{2,1,0:T(4,128)(2,1)}, u32[]{:S(2)}, u32[]{:S(2)}) async-start(bf16[32,4,2560]{2,1,0:T(4,128)(2,1)} %reshape.545), calls=%async_computation | async-start | bytes 1310720 | tf_op jit(solution)/shard_map/all_to_all | solution.py:116
  176.3 6.3 %copy-start.9 = (f32[128,4,5,128]{0,3,2,1:T(8,128)S(1)}, f32[128,4,5,128]{0,3,2,1:T(8,128)}, u32[]{:S(2)}) copy-start(f32[128,4,5,128]{0,3,2,1:T(8,128)} %convolution_bitcast_fusion.7) | copy-start | bytes 3932164
  176.3 6.3 %copy-start.10 = (f32[128,4,5,128]{0,3,2,1:T(8,128)S(1)}, f32[128,4,5,128]{0,3,2,1:T(8,128)}, u32[]{:S(2)}) copy-start(f32[128,4,5,128]{0,3,2,1:T(8,128)} %convolution_bitcast_fusion.5) | copy-start | bytes 3932164
  178.5 13.7 %collective-permute-start.11 = (bf16[128,1024]{1,0:T(8,128)(2,1)}, bf16[128,1024]{1,0:T(8,128)(2,1)}, u32[]{:S(2)}, u32[]{:S(2)}) collective-permute-start(bf16[128,1024]{1,0:T(8,128)(2,1)} %pad_maximum_fusion.6), channel_id=1, source_target_pairs={{0,3},{1,4},{2,5},{3,6},{4,7},{5,8},{6,9},{7,10},{8,11},{9,12},{10... | collective-permute-start | bytes 786440 | tf_op jit(solution)/shard_map/ppermute | solution.py:16
  183.1 9.0 %copy-start.33 = (bf16[128,512]{1,0:T(8,128)(2,1)S(1)}, bf16[128,512]{1,0:T(8,128)(2,1)}, u32[]{:S(2)}) copy-start(bf16[128,512]{1,0:T(8,128)(2,1)} %copy.242) | copy-start | bytes 393220
  183.1 9.0 %copy-start.34 = (bf16[128,512]{1,0:T(8,128)(2,1)S(1)}, bf16[128,512]{1,0:T(8,128)(2,1)}, u32[]{:S(2)}) copy-start(bf16[128,512]{1,0:T(8,128)(2,1)} %copy.241) | copy-start | bytes 393220
  (23 other events, 30.4 us)
where the time goes:
time: 202 us; the launch traced here: 199 us
  starting transfers between devices  66.4 us (33%)
  local copies, waits for them, and re-layouts  51.6 us (26%)
  matrix products  42.1 us (21%)
  other arithmetic  17.2 us (9%)
  between operations  13.3 us (7%)
  waiting for transfers between devices  8.46 us (4%)
    ppermute x12, starting transfers between devices, from_behind(): return lax.ppermute(x, axis, pairs)  43.8 us
    all_to_all x1, starting transfers between devices, body(): lax.all_to_all(out_grad[ffn_perm].reshape(device_count, peer_rows, out_gr...  11.3 us
    all_to_all x1, starting transfers between devices, body(): lax.all_to_all(attention_apply[att_perm].reshape(device_count, peer_rows,...  11.2 us
    reshape x7, local copies, waits for them, and re-layouts, body(): key_part.reshape(row_count, key_value_width)  10.7 us
    dot_general x7, matrix products, body(): jnp.einsum('hgqk,qhgd->khd', dscore, heads_of_query, preferred_element_ty...  10.5 us
    concatenate x6, other arithmetic, body(): jnp.concatenate([key_part.reshape(row_count, key_value_width), value_part...  10.1 us
    dot_general x7, matrix products, body(): jnp.einsum('hgqk,qhgd->khd', prob_b, head_gradient, preferred_element_typ...  8.98 us
    unnamed x118, local copies, waits for them, and re-layouts  8.81 us
  transfers between devices with their start and end apart: 14, of which 2 were waited for; matrix products, arithmetic and copies ran while one was open for 33% of the time, Pallas kernels for 0%

commit v1 on v0

v1 whole, which is shorter than its diff:
```python
import math

import jax
import jax.numpy as jnp
from jax import lax
from jax.experimental import pallas as pl
from jax.experimental.pallas import tpu as pltpu
from jax.sharding import PartitionSpec as P

MESH = pl.DeviceIdType.MESH
D = 128
HALF = 64
KV = 4
GR = 5
N = 32
CHUNK = 16
ROWS = N * CHUNK
WIDE = GR * D
KEYS = 4 * D
NEG = -1e30
CHUNKS = ((0, GR),)
BF, F32 = jnp.bfloat16, jnp.float32


def dot(a, b, ca, cb):
    return lax.dot_general(a, b, (((ca,), (cb,)), ((), ())), preferred_element_type=F32)


def iota(shape, dim):
    return lax.broadcasted_iota(jnp.int32, shape, dim)


def picks(c, ul):
    return (ul == ((c >> 2) & 3) * D + (c >> 4) * 4 + (c & 3)).astype(BF)


def scatter_matrix(orders):
    pick = picks(iota((KV * D, ROWS), 1), iota((KV * D, ROWS), 0))
    row, c = iota((D, ROWS), 0), iota((D, ROWS), 1)
    target = dot(orders, pick, 1, 0) + (((c >> 2) & 3) * D).astype(F32)
    row = row.astype(F32)
    return jnp.concatenate([(target == row + float(t * D)).astype(BF) for t in range(KV)], axis=0)


def gather_matrix(orders):
    pick = picks(iota((ROWS, KV * D), 0), iota((ROWS, KV * D), 1))
    c, lane = iota((ROWS, D), 0), iota((ROWS, D), 1)
    target = dot(pick, orders, 1, 1) + (((c >> 2) & 3) * D).astype(F32)
    lane = lane.astype(F32)
    return jnp.concatenate([(target == lane + float(t * D)).astype(BF) for t in range(KV)], axis=1)


def heads(x, lo=0, hi=GR):
    return jnp.concatenate([x[:, a * D : (a + 1) * D] for a in range(lo, hi)], axis=0)


def kernel(
    q_hbm, k_hbm, v_hbm, g_hbm, sizes_hbm, ffn_hbm, att_hbm,
    rcv2, qg, grow, gup, gdn, p_out,
    sizes, ffn_ref, att_ref, qb, kvb, qst, kvw, kall, prob, gin, snd1, rcv1, snd2,
    m_att, mt_att, ott, dos, dsb, dqs, accw, gsend, bias, flag,
    in_sem, att_s, att_r, kv_s, kv_r, q_s, q_r, dq_s, dq_r, g_s, g_r,
    a1_s, a1_r, a2_s, a2_r,
):
    dp = lax.axis_index("dp")
    me = lax.axis_index("ctx")
    z, x = me >> 2, me & 3
    above, below = ((z + 1) & 7) * KV, ((z + 7) & 7) * KV
    scale = 1.0 / math.sqrt(D)

    def remote(src, dst, s, r, peer):
        return pltpu.make_async_remote_copy(
            src_ref=src, dst_ref=dst, send_sem=s, recv_sem=r,
            device_id=(dp, peer), device_id_type=MESH,
        )

    def lanes(i, width):
        return pl.ds(pl.multiple_of(i * width, D), width)

    barrier = pltpu.get_barrier_semaphore()

    def greet(i, _):
        pl.semaphore_signal(
            barrier, inc=1, device_id=(dp, lax.rem(me + i, N)), device_id_type=MESH
        )
        return 0

    lax.fori_loop(1, N, greet, 0)

    local = [
        pltpu.make_async_copy(ffn_hbm, ffn_ref, in_sem.at[0]),
        pltpu.make_async_copy(g_hbm, gin, in_sem.at[1]),
        pltpu.make_async_copy(att_hbm, att_ref.at[x], in_sem.at[2]),
        pltpu.make_async_copy(sizes_hbm, sizes, in_sem.at[3]),
    ]
    for g in range(KV):
        cols = slice(g * D, (g + 1) * D)
        local += [
            pltpu.make_async_copy(k_hbm.at[:, cols], kvb.at[g, :, 0:D], in_sem.at[4 + 3 * g]),
            pltpu.make_async_copy(v_hbm.at[:, cols], kvb.at[g, :, D:], in_sem.at[5 + 3 * g]),
            pltpu.make_async_copy(
                q_hbm.at[:, g * WIDE : (g + 1) * WIDE], qb.at[g], in_sem.at[6 + 3 * g]
            ),
        ]
    for c in local:
        c.start()

    local[0].wait()
    order = ffn_ref[...].astype(F32)
    p_ffn = (order == iota((D, D), 0).astype(F32)).astype(BF)
    p_out[...] = p_ffn
    gather_ffn = p_ffn.T
    local[1].wait()
    for g in range(KV):
        snd1[g * D : (g + 1) * D, :] = dot(
            gather_ffn, gin[:, g * WIDE : (g + 1) * WIDE], 1, 0
        ).astype(BF)

    for c in local[2:]:
        c.wait()
    kvw[4 + x] = kvb[x]
    qst[x] = qb[x]

    pl.semaphore_wait(barrier, N - 1)

    def order_copy(i):
        return remote(att_ref.at[x], att_ref.at[x], att_s.at[i], att_r.at[i], z * KV + ((x + i) & 3))

    def order_arrived(i):
        u = (x + 4 - i) & 3
        return remote(att_ref.at[u], att_ref.at[u], att_s.at[i], att_r.at[i], me ^ 1)

    for i in (1, 2, 3):
        order_copy(i).start()

    def kv_copy(i, what):
        g = (x + i) & 3
        s = kv_s.at[i, what]
        if what == 0:
            return remote(kvb.at[g], kvw.at[4 + x], s, kv_r.at[4 + x], z * KV + g)
        if what == 1:
            return remote(kvb.at[g], kvw.at[8 + x], s, kv_r.at[8 + x], below + g)
        return remote(kvb.at[g, 0:HALF], kvw.at[x, 0:HALF], s, kv_r.at[x], above + g)

    def kv_all(action):
        for i in (2, 1, 3):
            action(kv_copy(i, 0))
        for i in (2, 1, 3, 0):

            @pl.when(x <= 2)
            def _():
                action(kv_copy(i, 1))

            @pl.when(x >= 1)
            def _():
                action(kv_copy(i, 2))

    kv_all(lambda c: c.start())

    def q_copy(i):
        g = (x + i) & 3
        return remote(qb.at[g], qst.at[x], q_s.at[i], q_r.at[x], z * KV + g)

    for i in (2, 1, 3):
        q_copy(i).start()

    def rows_at(i):
        return pl.ds(pl.multiple_of(i * CHUNK, CHUNK), CHUNK)

    def token_row(peer):
        return pl.ds(pl.multiple_of((peer & 3) * D + (peer >> 2) * CHUNK, CHUNK), CHUNK)

    def send1(i, _):
        peer = lax.rem(me + i, N)
        remote(snd1.at[token_row(peer)], rcv1.at[rows_at(me)], a1_s, a1_r, peer).start()
        return 0

    lax.fori_loop(1, N, send1, 0)
    rcv1[rows_at(me), :] = snd1[token_row(me), :]

    def whole(src, dst, s, r):
        n = ROWS - CHUNK
        return remote(src.at[:n], dst.at[:n], s, r, lax.rem(me + 1, N))

    kk, qq = iota((D, D), 0), iota((D, D), 1)
    for u in range(KV):
        d = z * KV + u
        first, end, start = 0, 0, 0
        for t in range(16):
            stop = start + sizes[t]
            inside = (start <= d) & (d < stop)
            first = jnp.where(inside, start, first)
            end = jnp.where(inside, stop, end)
            start = stop
        bias[u, 0:D, :] = jnp.where(kk <= qq, 0.0, NEG)
        for r in (1, 2, 3):
            flag[u * KV + r] = jnp.where(d + r < end, 1, 0)
            later = jnp.where(d + r < end, 0.0, NEG)
            earlier = jnp.where(d + r - 4 >= first, 0.0, NEG)
            bias[u, r * D : (r + 1) * D, :] = jnp.maximum(
                jnp.where(qq >= HALF, later, NEG), jnp.where(kk < HALF, earlier, NEG)
            )
    accw[...] = jnp.zeros_like(accw)

    for i in (1, 2, 3):
        order_arrived(i).wait_recv()
    orders = jnp.concatenate([att_ref[u] for u in range(KV)], axis=1)
    orders = jnp.broadcast_to(orders.astype(F32).astype(BF), (D, KV * D))
    m_att[...] = scatter_matrix(orders)
    mt_att[...] = gather_matrix(orders)

    for e in range(1, 11):
        rows = slice(0, HALF) if e < 4 else slice(0, D)
        c = remote(kvb.at[0, rows], kvw.at[e, rows], kv_s.at[0, 0], kv_r.at[e], me ^ 1)
        if 4 <= e < 8:
            pl.when(x != e - 4)(c.wait_recv)
        else:
            c.wait_recv()

    def forward(i, _):
        u = (x + i) & 3

        @pl.when(i > 0)
        def _():
            remote(qb.at[0], qst.at[u], q_s.at[0], q_r.at[u], me ^ 1).wait_recv()

        kall[u, 0:D, :] = kvw[4 + u]
        for r in (1, 2, 3):
            kall[u, r * D : r * D + HALF, :] = jnp.where(
                flag[u * KV + r] > 0, kvw[4 + u + r, 0:HALF, :], kvw[u + r, 0:HALF, :]
            )
            kall[u, r * D + HALF : (r + 1) * D, :] = kvw[4 + u + r, HALF:D, :]
        keys, values = kall[u, :, 0:D], kall[u, :, D : 2 * D]
        values_t = values.T
        c = scale * math.log2(math.e)
        for lo, hi in CHUNKS:
            s = dot(keys, heads(qst[u], lo, hi), 1, 1)
            s = s + jnp.concatenate([bias[u]] * (hi - lo), axis=1)
            top = jnp.max(s, axis=0, keepdims=True)
            p = jnp.exp2(s * c - top * c)
            p = (p * (1.0 / jnp.sum(p, axis=0, keepdims=True))).astype(BF)
            prob[u, :, lo * D : hi * D] = p
            o = dot(values_t, p, 1, 0).astype(BF)
            for a in range(lo, hi):
                ott[a * D : (a + 1) * D, lanes(u, D)] = o[:, (a - lo) * D : (a - lo + 1) * D]
        return 0

    lax.fori_loop(0, KV, forward, 0)

    snd2[...] = dot(mt_att[...], ott[...], 1, 1).astype(BF)

    def send2(i, _):
        peer = lax.rem(me + i, N)
        remote(snd2.at[rows_at(peer)], rcv2.at[token_row(me)], a2_s, a2_r, peer).start()
        return 0

    lax.fori_loop(1, N, send2, 0)
    rcv2[token_row(me), :] = snd2[rows_at(me), :]

    whole(snd1, rcv1, a1_s, a1_r).wait_recv()
    for u in range(KV):
        dos[u] = dot(m_att[u * D : (u + 1) * D, :], rcv1[...], 1, 0).astype(BF)

    def dq_copy(u):
        return remote(dqs.at[u], qg.at[x], dq_s.at[u], dq_r.at[x], z * KV + u)

    def backward(i, _):
        u = (x + 1 + i) & 3
        keys, values = kall[u, :, 0:D], kall[u, :, D : 2 * D]
        keys_t = keys.T
        for lo, hi in CHUNKS:
            dp_t = dot(values, heads(dos[u], lo, hi), 1, 1)
            pf = prob[u, :, lo * D : hi * D].astype(F32)
            t = pf * dp_t
            ds = (t - pf * jnp.sum(t, axis=0, keepdims=True)).astype(BF)
            dsb[:, lo * D : hi * D] = ds
            dq = dot(keys_t, ds, 1, 0) * scale
            for a in range(lo, hi):
                dqs[u, :, a * D : (a + 1) * D] = (
                    dq[:, (a - lo) * D : (a - lo + 1) * D].T.astype(BF)
                )

        @pl.when(i < 3)
        def _():
            dq_copy(u).start()

        kpart = dot(dsb[...], heads(qst[u]), 1, 0) * scale
        vpart = dot(prob[u], heads(dos[u]), 1, 0)
        part = jnp.concatenate([kpart, vpart], axis=1)
        accw[4 + u] += part[0:D]
        for r in (1, 2, 3):
            later = flag[u * KV + r] > 0
            accw[4 + u + r] += jnp.where(later, part[r * D : (r + 1) * D], 0.0)
            accw[u + r, 0:HALF, :] += jnp.where(later, 0.0, part[r * D : r * D + HALF])
        return 0

    lax.fori_loop(0, KV, backward, 0)
    qg[x] = dqs[x]

    for e in range(1, 11):
        gsend[e] = accw[e].astype(BF)

    def g_copy(e):
        g = e & 3
        if e < 4:
            return remote(gsend.at[e, 0:HALF], gdn.at[x], g_s.at[e], g_r.at[0, x], below + g)
        if e < 8:
            return remote(gsend.at[e], grow.at[x], g_s.at[e], g_r.at[1, x], z * KV + g)
        return remote(gsend.at[e], gup.at[x], g_s.at[e], g_r.at[2, x], above + g)

    for e in (8, 9, 10, 1, 2, 3):
        g_copy(e).start()
    for e in range(4, 8):
        pl.when(x != e - 4)(g_copy(e).start)
    grow[x] = gsend[4 + x]

    whole(snd2, rcv2, a2_s, a2_r).wait_recv()
    for g in range(KV):
        pl.when(x != g)(
            remote(gsend.at[4], grow.at[g], g_s.at[0], g_r.at[1, g], me ^ 1).wait_recv
        )
        pl.when(x <= 2)(remote(gsend.at[4], gup.at[g], g_s.at[0], g_r.at[2, g], me ^ 1).wait_recv)
        pl.when(x >= 1)(
            remote(gsend.at[4, 0:HALF], gdn.at[g], g_s.at[0], g_r.at[0, g], me ^ 1).wait_recv
        )

    for i in (1, 2, 3):
        order_copy(i).wait_send()
        q_copy(i).wait_send()
    kv_all(lambda c: c.wait_send())
    whole(snd1, rcv1, a1_s, a1_r).wait_send()
    whole(snd2, rcv2, a2_s, a2_r).wait_send()
    for e in (8, 9, 10, 1, 2, 3):
        g_copy(e).wait_send()
    for u in range(KV):

        @pl.when(x != u)
        def _():
            g_copy(4 + u).wait_send()
            dq_copy(u).wait_send()
            remote(dqs.at[u], qg.at[u], dq_s.at[u], dq_r.at[u], me ^ 1).wait_recv()


def finish(
    got, qg, grow, gup, gdn, p_ffn,
    out_hbm, qg_hbm, kg_hbm, vg_hbm,
    out_v, kg_v, vg_v, sem,
):
    x = lax.axis_index("ctx") & 3
    outs = []

    def send(src, dst):
        outs.append(pltpu.make_async_copy(src, dst, sem.at[len(outs)]))
        outs[-1].start()

    for g in range(KV):
        send(qg.at[g], qg_hbm.at[:, g * WIDE : (g + 1) * WIDE])
    for g in range(KV):
        total = grow[g].astype(F32) + jnp.where(x <= 2, gup[g].astype(F32), 0.0)
        low = total[0:HALF] + jnp.where(x >= 1, gdn[g].astype(F32), 0.0)
        high = total[HALF:D]
        cols = slice(g * D, (g + 1) * D)
        for ref, lane in ((kg_v, 0), (vg_v, D)):
            ref[0:HALF, cols] = low[:, lane : lane + D].astype(BF)
            ref[HALF:D, cols] = high[:, lane : lane + D].astype(BF)
    send(kg_v, kg_hbm)
    send(vg_v, vg_hbm)
    for g in range(KV):
        cols = slice(g * WIDE, (g + 1) * WIDE)
        out_v[:, cols] = dot(p_ffn[...], got[g * D : (g + 1) * D, :], 1, 0).astype(BF)
        send(out_v.at[:, cols], out_hbm.at[:, cols])
    for c in outs:
        c.wait()


def body(q, k, v, g, sizes, ffn_order, attn_order):
    hbm = pl.BlockSpec(memory_space=pltpu.HBM)
    vmem = pl.BlockSpec(memory_space=pltpu.VMEM)
    dma = pltpu.SemaphoreType.DMA
    vm = pltpu.VMEM
    got, qg, row, up, down, p_ffn = pl.pallas_call(
        kernel,
        out_shape=(
            vm((ROWS, WIDE), BF),
            vm((KV, D, WIDE), BF),
            vm((KV, D, 2 * D), BF),
            vm((KV, D, 2 * D), BF),
            vm((KV, HALF, 2 * D), BF),
            vm((D, D), BF),
        ),
        in_specs=[hbm] * 7,
        out_specs=(vmem,) * 6,
        scratch_shapes=[
            pltpu.SMEM((16,), jnp.int32),
            vm((1, D), jnp.int32),
            vm((KV, 1, D), jnp.int32),
            vm((KV, D, WIDE), BF),
            vm((KV, D, 2 * D), BF),
            vm((KV, D, WIDE), BF),
            vm((12, D, 2 * D), BF),
            vm((KV, KEYS, 2 * D), BF),
            vm((KV, KEYS, WIDE), BF),
            vm((D, KV * WIDE), BF),
            vm((ROWS, WIDE), BF),
            vm((ROWS, WIDE), BF),
            vm((ROWS, WIDE), BF),
            vm((KV * D, ROWS), BF),
            vm((ROWS, KV * D), BF),
            vm((WIDE, KV * D), BF),
            vm((KV, D, WIDE), BF),
            vm((KEYS, WIDE), BF),
            vm((KV, D, WIDE), BF),
            vm((12, D, 2 * D), F32),
            vm((12, D, 2 * D), BF),
            vm((KV, KEYS, D), F32),
            pltpu.SMEM((KV * KV,), jnp.int32),
            dma((16,)),
            dma((4,)),
            dma((4,)),
            dma((4, 3)),
            dma((12,)),
            dma((4,)),
            dma((4,)),
            dma((4,)),
            dma((4,)),
            dma((12,)),
            dma((3, 4)),
            dma,
            dma,
            dma,
            dma,
        ],
        compiler_params=pltpu.CompilerParams(
            collective_id=0, has_side_effects=True, vmem_limit_bytes=56 * 1024 * 1024
        ),
    )(q, k, v, g, sizes, ffn_order, attn_order)
    return pl.pallas_call(
        finish,
        out_shape=(
            jax.ShapeDtypeStruct((D, KV * WIDE), BF),
            jax.ShapeDtypeStruct((D, KV * WIDE), BF),
            jax.ShapeDtypeStruct((D, KV * D), BF),
            jax.ShapeDtypeStruct((D, KV * D), BF),
        ),
        in_specs=[vmem] * 6,
        out_specs=(hbm,) * 4,
        scratch_shapes=[
            vm((D, KV * WIDE), BF),
            vm((D, KV * D), BF),
            vm((D, KV * D), BF),
            dma((10,)),
        ],
        compiler_params=pltpu.CompilerParams(vmem_limit_bytes=8 * 1024 * 1024),
    )(got, qg, row, up, down, p_ffn)


def solution(mesh):
    rows = P(("dp", "ctx"), None)
    return jax.shard_map(
        body,
        mesh=mesh,
        in_specs=(rows, rows, rows, rows, P("dp"), rows, rows),
        out_specs=(rows,) * 4,
        check_vma=False,
    )
```

time: 202 us -> 60 us (0.30); the launches traced: 199 us -> 59.4 us
  starting transfers between devices: 66.4 us -> 0 us
  Pallas kernels: 0 us -> 58.7 us
  local copies, waits for them, and re-layouts: 51.6 us -> 0 us
  matrix products: 42.1 us -> 0 us
  other arithmetic: 17.2 us -> 0 us
  between operations: 13.3 us -> 0.64 us
  waiting for transfers between devices: 8.46 us -> 0 us
    pallas_call x0 -> x2, Pallas kernels: none -> 58.7 us  [the longest x1 57.5 us: body(): pl.pallas_call(kernel, out_shape=(vm((ROWS, WIDE), BF), vm((KV, D, WIDE),...]
    ppermute x12 -> x0, starting transfers between devices: 43.8 us -> none  [from_behind(): return lax.ppermute(x, axis, pairs)]
    dot_general x42 -> x0, matrix products: 42.1 us -> none  [the longest x7 10.5 us: body(): jnp.einsum('hgqk,qhgd->khd', dscore, heads_of_query, preferred_element_ty...]
    reshape x21 -> x0, local copies, waits for them, and re-layouts: 25.7 us -> none  [the longest x7 10.7 us: body(): key_part.reshape(row_count, key_value_width)]
    all_to_all x2 -> x0, starting transfers between devices: 22.5 us -> none  [the longest x1 11.3 us: body(): lax.all_to_all(out_grad[ffn_perm].reshape(device_count, peer_rows, out_gr...]
    concatenate x7 -> x0, other arithmetic: 10.8 us -> none  [the longest x6 10.1 us: body(): jnp.concatenate([key_part.reshape(row_count, key_value_width), value_part...]
    unnamed x118 -> x0, local copies, waits for them, and re-layouts: 8.81 us -> none
    ppermute x12 -> x0, waiting for transfers between devices: 7.94 us -> none  [from_behind(): return lax.ppermute(x, axis, pairs)]
  transfers between devices with their start and end apart: 14 -> 0, of which waited for: 2 -> 0; matrix products, arithmetic and copies ran while one was open for 33% -> 0% of each run, Pallas kernels for 0% -> 0%
where the time goes in v1:
time: 60 us; the launch traced here: 59.4 us
  Pallas kernels  58.7 us (98%)
  between operations  0.64 us (1%)
    pallas_call x1, Pallas kernels, body(): pl.pallas_call(kernel, out_shape=(vm((ROWS, WIDE), BF), vm((KV, D, WIDE),...  57.5 us
    pallas_call x1, Pallas kernels, body(): pl.pallas_call(finish, out_shape=(jax.ShapeDtypeStruct((D, KV * WIDE), BF...  1.24 us

profile of v1, /device:TPU:2, one launch (start us, length us, event | category | flops | bytes accessed | tf_op | source)
XLA Modules:
  0.0 59.4 jit_solution(6500531452322467837)
XLA Ops:
  0.6 57.5 %shard_map.102 = (bf16[512,640]{1,0:T(8,128)(2,1)S(1)}, bf16[4,128,640]{2,1,0:T(8,128)(2,1)S(1)}, bf16[4,128,256]{2,1,0:T(8,128)(2,1)S(1)}, bf16[4,128,256]{2,1,...) custom-call(bf16[128,2560]{1,0:T(8,128)(2,1)} %q_hbm.1, bf16[128,512]{1,0:T(8,128)(2,1)} %k_hbm.1, ...), custom_call_target="tpu_custom_call" | custom-call | tf_op jit(solution)/shard_map/pallas_call | solution.py:381
  58.1 1.2 %shard_map.103 = (bf16[128,2560]{1,0:T(8,128)(2,1)}, bf16[128,2560]{1,0:T(8,128)(2,1)}, bf16[128,512]{1,0:T(8,128)(2,1)}, bf16[128,512]{1,0:T(8,128)(2,1)}) custom-call(bf16[512,640]{1,0:T(8,128)(2,1)S(1)} %get-tuple-element.10.got, bf16[4,128,640]{2,1,0:T(8,128)(2,1)S(1)} %get-tuple-element.11.qg, bf16[4,128,256]{2,1,0:T(8,128)(2,1)S(1)} %get-tuple-element.12.grow, ...), custom_call_target="tpu_custom_call" | custom-call | tf_op jit(solution)/shard_map/pallas_call | solution.py:437

commit v2 on v1

--- a/solution.py
+++ b/solution.py
@@ -18,7 +18,7 @@
 WIDE = GR * D
 KEYS = 4 * D
 NEG = -1e30
-CHUNKS = ((0, GR),)
+STEP = 32
 BF, F32 = jnp.bfloat16, jnp.float32
 
 
@@ -50,15 +50,15 @@
     return jnp.concatenate([(target == lane + float(t * D)).astype(BF) for t in range(KV)], axis=1)
 
 
-def heads(x, lo=0, hi=GR):
-    return jnp.concatenate([x[:, a * D : (a + 1) * D] for a in range(lo, hi)], axis=0)
+def heads(x):
+    return jnp.concatenate([x[:, a * D : (a + 1) * D] for a in range(GR)], axis=0)
 
 
 def kernel(
     q_hbm, k_hbm, v_hbm, g_hbm, sizes_hbm, ffn_hbm, att_hbm,
     rcv2, qg, grow, gup, gdn, p_out,
     sizes, ffn_ref, att_ref, qb, kvb, qst, kvw, kall, prob, gin, snd1, rcv1, snd2,
-    m_att, mt_att, ott, dos, dsb, dqs, accw, gsend, bias, flag,
+    m_att, mt_att, ott, dos, sc, dsb, dqs, accw, gsend, bias, invs, flag,
     in_sem, att_s, att_r, kv_s, kv_r, q_s, q_r, dq_s, dq_r, g_s, g_r,
     a1_s, a1_r, a2_s, a2_r,
 ):
@@ -102,19 +102,8 @@
                 q_hbm.at[:, g * WIDE : (g + 1) * WIDE], qb.at[g], in_sem.at[6 + 3 * g]
             ),
         ]
-    for c in local:
+    for c in local[4:] + local[:4]:
         c.start()
-
-    local[0].wait()
-    order = ffn_ref[...].astype(F32)
-    p_ffn = (order == iota((D, D), 0).astype(F32)).astype(BF)
-    p_out[...] = p_ffn
-    gather_ffn = p_ffn.T
-    local[1].wait()
-    for g in range(KV):
-        snd1[g * D : (g + 1) * D, :] = dot(
-            gather_ffn, gin[:, g * WIDE : (g + 1) * WIDE], 1, 0
-        ).astype(BF)
 
     for c in local[2:]:
         c.wait()
@@ -163,6 +152,16 @@
 
     for i in (2, 1, 3):
         q_copy(i).start()
+
+    local[0].wait()
+    order = ffn_ref[...].astype(F32)
+    p_ffn = (order == iota((D, D), 0).astype(F32)).astype(BF)
+    p_out[...] = p_ffn
+    gather_ffn = p_ffn.T
+    local[1].wait()
+    packed = dot(gather_ffn, gin[...], 1, 0).astype(BF)
+    for g in range(KV):
+        snd1[g * D : (g + 1) * D, :] = packed[:, g * WIDE : (g + 1) * WIDE]
 
     def rows_at(i):
         return pl.ds(pl.multiple_of(i * CHUNK, CHUNK), CHUNK)
@@ -201,6 +200,7 @@
                 jnp.where(qq >= HALF, later, NEG), jnp.where(kk < HALF, earlier, NEG)
             )
     accw[...] = jnp.zeros_like(accw)
+    invs[...] = jnp.zeros_like(invs)
 
     for i in (1, 2, 3):
         order_arrived(i).wait_recv()
@@ -231,18 +231,30 @@
             )
             kall[u, r * D + HALF : (r + 1) * D, :] = kvw[4 + u + r, HALF:D, :]
         keys, values = kall[u, :, 0:D], kall[u, :, D : 2 * D]
-        values_t = values.T
-        c = scale * math.log2(math.e)
-        for lo, hi in CHUNKS:
-            s = dot(keys, heads(qst[u], lo, hi), 1, 1)
-            s = s + jnp.concatenate([bias[u]] * (hi - lo), axis=1)
-            top = jnp.max(s, axis=0, keepdims=True)
-            p = jnp.exp2(s * c - top * c)
-            p = (p * (1.0 / jnp.sum(p, axis=0, keepdims=True))).astype(BF)
-            prob[u, :, lo * D : hi * D] = p
-            o = dot(values_t, p, 1, 0).astype(BF)
-            for a in range(lo, hi):
-                ott[a * D : (a + 1) * D, lanes(u, D)] = o[:, (a - lo) * D : (a - lo + 1) * D]
+        sc[...] = dot(keys, heads(qst[u]), 1, 1)
+
+        def masked(b):
+            rows = pl.ds(pl.multiple_of(b * STEP, STEP), STEP)
+            return sc[rows, :] + jnp.concatenate([bias[u, rows, :]] * GR, axis=1)
+
+        def largest(b, top):
+            return jnp.maximum(top, jnp.max(masked(b).reshape(STEP // 8, 8, WIDE), axis=0))
+
+        top = lax.fori_loop(0, KEYS // STEP, largest, jnp.full((8, WIDE), NEG, F32))
+        top = jnp.max(top, axis=0, keepdims=True)
+
+        def weigh(b, total):
+            p = jnp.exp2((masked(b) - top) * (scale * math.log2(math.e)))
+            prob[u, pl.ds(pl.multiple_of(b * STEP, STEP), STEP), :] = p.astype(BF)
+            return total + jnp.sum(p.reshape(STEP // 8, 8, WIDE), axis=0)
+
+        total = lax.fori_loop(0, KEYS // STEP, weigh, jnp.zeros((8, WIDE), F32))
+        inv = 1.0 / jnp.sum(total, axis=0, keepdims=True)
+        o = (dot(values.T, prob[u], 1, 0) * inv).astype(BF)
+        for a in range(GR):
+            cols = slice(a * D, (a + 1) * D)
+            ott[cols, lanes(u, D)] = o[:, cols]
+            invs[u, a : a + 1, :] = inv[:, cols]
         return 0
 
     lax.fori_loop(0, KV, forward, 0)
@@ -259,7 +271,11 @@
 
     whole(snd1, rcv1, a1_s, a1_r).wait_recv()
     for u in range(KV):
-        dos[u] = dot(m_att[u * D : (u + 1) * D, :], rcv1[...], 1, 0).astype(BF)
+        up = dot(m_att[u * D : (u + 1) * D, :], rcv1[...], 1, 0)
+        inv = invs[u].T
+        for a in range(GR):
+            cols = slice(a * D, (a + 1) * D)
+            dos[u, :, cols] = (up[:, cols] * inv[:, a : a + 1]).astype(BF)
 
     def dq_copy(u):
         return remote(dqs.at[u], qg.at[x], dq_s.at[u], dq_r.at[x], z * KV + u)
@@ -267,18 +283,30 @@
     def backward(i, _):
         u = (x + 1 + i) & 3
         keys, values = kall[u, :, 0:D], kall[u, :, D : 2 * D]
-        keys_t = keys.T
-        for lo, hi in CHUNKS:
-            dp_t = dot(values, heads(dos[u], lo, hi), 1, 1)
-            pf = prob[u, :, lo * D : hi * D].astype(F32)
-            t = pf * dp_t
-            ds = (t - pf * jnp.sum(t, axis=0, keepdims=True)).astype(BF)
-            dsb[:, lo * D : hi * D] = ds
-            dq = dot(keys_t, ds, 1, 0) * scale
-            for a in range(lo, hi):
-                dqs[u, :, a * D : (a + 1) * D] = (
-                    dq[:, (a - lo) * D : (a - lo + 1) * D].T.astype(BF)
-                )
+        sc[...] = dot(values, heads(dos[u]), 1, 1)
+
+        def blocks(b):
+            rows = pl.ds(pl.multiple_of(b * STEP, STEP), STEP)
+            return prob[u, rows, :].astype(F32), sc[rows, :]
+
+        def add(b, total):
+            p, dp_t = blocks(b)
+            return total + jnp.sum((p * dp_t).reshape(STEP // 8, 8, WIDE), axis=0)
+
+        total = lax.fori_loop(0, KEYS // STEP, add, jnp.zeros((8, WIDE), F32))
+        inv = jnp.concatenate([invs[u, a : a + 1, :] for a in range(GR)], axis=1)
+        delta = jnp.sum(total, axis=0, keepdims=True) * inv
+
+        def score(b, _):
+            p, dp_t = blocks(b)
+            dsb[pl.ds(pl.multiple_of(b * STEP, STEP), STEP), :] = (p * (dp_t - delta)).astype(BF)
+            return 0
+
+        lax.fori_loop(0, KEYS // STEP, score, 0)
+        dq = dot(keys.T, dsb[...], 1, 0) * scale
+        for a in range(GR):
+            cols = slice(a * D, (a + 1) * D)
+            dqs[u, :, cols] = dq[:, cols].T.astype(BF)
 
         @pl.when(i < 3)
         def _():
@@ -408,11 +436,13 @@
             vm((ROWS, KV * D), BF),
             vm((WIDE, KV * D), BF),
             vm((KV, D, WIDE), BF),
+            vm((KEYS, WIDE), F32),
             vm((KEYS, WIDE), BF),
             vm((KV, D, WIDE), BF),
             vm((12, D, 2 * D), F32),
             vm((12, D, 2 * D), BF),
             vm((KV, KEYS, D), F32),
+            vm((KV, 8, D), F32),
             pltpu.SMEM((KV * KV,), jnp.int32),
             dma((16,)),
             dma((4,)),

time: 60 us -> 61.5 us (1.025)
  Pallas kernels: 58.7 us -> 60.8 us
    pallas_call x1, Pallas kernels: 57.5 us -> 59.5 us  [body(): pl.pallas_call(kernel, out_shape=(vm((ROWS, WIDE), BF), vm((KV, D, WIDE),...]
where the time goes in v2:
time: 61.5 us; the launch traced here: 61.4 us
  Pallas kernels  60.8 us (99%)
  between operations  0.64 us (1%)
    pallas_call x1, Pallas kernels, body(): pl.pallas_call(kernel, out_shape=(vm((ROWS, WIDE), BF), vm((KV, D, WIDE),...  59.5 us
    pallas_call x1, Pallas kernels, body(): pl.pallas_call(finish, out_shape=(jax.ShapeDtypeStruct((D, KV * WIDE), BF...  1.24 us

profile of v2, /device:TPU:2, one launch (start us, length us, event | category | flops | bytes accessed | tf_op | source)
XLA Modules:
  0.0 61.4 jit_solution(10536395276562904754)
XLA Ops:
  0.6 59.5 %shard_map.102 = (bf16[512,640]{1,0:T(8,128)(2,1)S(1)}, bf16[4,128,640]{2,1,0:T(8,128)(2,1)S(1)}, bf16[4,128,256]{2,1,0:T(8,128)(2,1)S(1)}, bf16[4,128,256]{2,1,...) custom-call(bf16[128,2560]{1,0:T(8,128)(2,1)} %q_hbm.1, bf16[128,512]{1,0:T(8,128)(2,1)} %k_hbm.1, ...), custom_call_target="tpu_custom_call" | custom-call | tf_op jit(solution)/shard_map/pallas_call | solution.py:409
  60.2 1.2 %shard_map.103 = (bf16[128,2560]{1,0:T(8,128)(2,1)}, bf16[128,2560]{1,0:T(8,128)(2,1)}, bf16[128,512]{1,0:T(8,128)(2,1)}, bf16[128,512]{1,0:T(8,128)(2,1)}) custom-call(bf16[512,640]{1,0:T(8,128)(2,1)S(1)} %get-tuple-element.10.got, bf16[4,128,640]{2,1,0:T(8,128)(2,1)S(1)} %get-tuple-element.11.qg, bf16[4,128,256]{2,1,0:T(8,128)(2,1)S(1)} %get-tuple-element.12.grow, ...), custom_call_target="tpu_custom_call" | custom-call | tf_op jit(solution)/shard_map/pallas_call | solution.py:467

commit v3 on v2

--- a/solution.py
+++ b/solution.py
@@ -18,6 +18,7 @@
 WIDE = GR * D
 KEYS = 4 * D
 NEG = -1e30
+TURN = 13
 STEP = 32
 BF, F32 = jnp.bfloat16, jnp.float32
 
@@ -105,6 +106,16 @@
     for c in local[4:] + local[:4]:
         c.start()
 
+    local[0].wait()
+    order = ffn_ref[...].astype(F32)
+    p_ffn = (order == iota((D, D), 0).astype(F32)).astype(BF)
+    p_out[...] = p_ffn
+    gather_ffn = p_ffn.T
+    local[1].wait()
+    packed = dot(gather_ffn, gin[...], 1, 0).astype(BF)
+    for g in range(KV):
+        snd1[g * D : (g + 1) * D, :] = packed[:, g * WIDE : (g + 1) * WIDE]
+
     for c in local[2:]:
         c.wait()
     kvw[4 + x] = kvb[x]
@@ -153,16 +164,6 @@
     for i in (2, 1, 3):
         q_copy(i).start()
 
-    local[0].wait()
-    order = ffn_ref[...].astype(F32)
-    p_ffn = (order == iota((D, D), 0).astype(F32)).astype(BF)
-    p_out[...] = p_ffn
-    gather_ffn = p_ffn.T
-    local[1].wait()
-    packed = dot(gather_ffn, gin[...], 1, 0).astype(BF)
-    for g in range(KV):
-        snd1[g * D : (g + 1) * D, :] = packed[:, g * WIDE : (g + 1) * WIDE]
-
     def rows_at(i):
         return pl.ds(pl.multiple_of(i * CHUNK, CHUNK), CHUNK)
 
@@ -170,7 +171,7 @@
         return pl.ds(pl.multiple_of((peer & 3) * D + (peer >> 2) * CHUNK, CHUNK), CHUNK)
 
     def send1(i, _):
-        peer = lax.rem(me + i, N)
+        peer = (me + TURN * i) & (N - 1)
         remote(snd1.at[token_row(peer)], rcv1.at[rows_at(me)], a1_s, a1_r, peer).start()
         return 0
 
@@ -262,7 +263,7 @@
     snd2[...] = dot(mt_att[...], ott[...], 1, 1).astype(BF)
 
     def send2(i, _):
-        peer = lax.rem(me + i, N)
+        peer = (me + TURN * i) & (N - 1)
         remote(snd2.at[rows_at(peer)], rcv2.at[token_row(me)], a2_s, a2_r, peer).start()
         return 0
 

time: 61.5 us -> 61.9 us (level)
  no operation moved by 1% of the time
where the time goes in v3:
time: 61.9 us; the launch traced here: 61.7 us
  Pallas kernels  61 us (99%)
  between operations  0.64 us (1%)
    pallas_call x1, Pallas kernels, body(): pl.pallas_call(kernel, out_shape=(vm((ROWS, WIDE), BF), vm((KV, D, WIDE),...  59.8 us

profile of v3, /device:TPU:2, one launch (start us, length us, event | category | flops | bytes accessed | tf_op | source)
XLA Modules:
  0.0 61.7 jit_solution(12456051514873846074)
XLA Ops:
  0.6 59.8 %shard_map.102 = (bf16[512,640]{1,0:T(8,128)(2,1)S(1)}, bf16[4,128,640]{2,1,0:T(8,128)(2,1)S(1)}, bf16[4,128,256]{2,1,0:T(8,128)(2,1)S(1)}, bf16[4,128,256]{2,1,...) custom-call(bf16[128,2560]{1,0:T(8,128)(2,1)} %q_hbm.1, bf16[128,512]{1,0:T(8,128)(2,1)} %k_hbm.1, ...), custom_call_target="tpu_custom_call" | custom-call | tf_op jit(solution)/shard_map/pallas_call | solution.py:410
  60.4 1.2 %shard_map.103 = (bf16[128,2560]{1,0:T(8,128)(2,1)}, bf16[128,2560]{1,0:T(8,128)(2,1)}, bf16[128,512]{1,0:T(8,128)(2,1)}, bf16[128,512]{1,0:T(8,128)(2,1)}) custom-call(bf16[512,640]{1,0:T(8,128)(2,1)S(1)} %get-tuple-element.10.got, bf16[4,128,640]{2,1,0:T(8,128)(2,1)S(1)} %get-tuple-element.11.qg, bf16[4,128,256]{2,1,0:T(8,128)(2,1)S(1)} %get-tuple-element.12.grow, ...), custom_call_target="tpu_custom_call" | custom-call | tf_op jit(solution)/shard_map/pallas_call | solution.py:468

commit v4 on v3

--- a/solution.py
+++ b/solution.py
@@ -234,22 +234,20 @@
         keys, values = kall[u, :, 0:D], kall[u, :, D : 2 * D]
         sc[...] = dot(keys, heads(qst[u]), 1, 1)
 
-        def masked(b):
-            rows = pl.ds(pl.multiple_of(b * STEP, STEP), STEP)
+        blocks = [slice(b, b + STEP) for b in range(0, KEYS, STEP)]
+
+        def masked(rows):
             return sc[rows, :] + jnp.concatenate([bias[u, rows, :]] * GR, axis=1)
 
-        def largest(b, top):
-            return jnp.maximum(top, jnp.max(masked(b).reshape(STEP // 8, 8, WIDE), axis=0))
-
-        top = lax.fori_loop(0, KEYS // STEP, largest, jnp.full((8, WIDE), NEG, F32))
+        top = jnp.full((8, WIDE), NEG, F32)
+        for rows in blocks:
+            top = jnp.maximum(top, jnp.max(masked(rows).reshape(STEP // 8, 8, WIDE), axis=0))
         top = jnp.max(top, axis=0, keepdims=True)
-
-        def weigh(b, total):
-            p = jnp.exp2((masked(b) - top) * (scale * math.log2(math.e)))
-            prob[u, pl.ds(pl.multiple_of(b * STEP, STEP), STEP), :] = p.astype(BF)
-            return total + jnp.sum(p.reshape(STEP // 8, 8, WIDE), axis=0)
-
-        total = lax.fori_loop(0, KEYS // STEP, weigh, jnp.zeros((8, WIDE), F32))
+        total = jnp.zeros((8, WIDE), F32)
+        for rows in blocks:
+            p = jnp.exp2((masked(rows) - top) * (scale * math.log2(math.e)))
+            prob[u, rows, :] = p.astype(BF)
+            total = total + jnp.sum(p.reshape(STEP // 8, 8, WIDE), axis=0)
         inv = 1.0 / jnp.sum(total, axis=0, keepdims=True)
         o = (dot(values.T, prob[u], 1, 0) * inv).astype(BF)
         for a in range(GR):
@@ -271,8 +269,9 @@
     rcv2[token_row(me), :] = snd2[rows_at(me), :]
 
     whole(snd1, rcv1, a1_s, a1_r).wait_recv()
+    every = dot(m_att[...], rcv1[...], 1, 0)
     for u in range(KV):
-        up = dot(m_att[u * D : (u + 1) * D, :], rcv1[...], 1, 0)
+        up = every[u * D : (u + 1) * D]
         inv = invs[u].T
         for a in range(GR):
             cols = slice(a * D, (a + 1) * D)
@@ -286,24 +285,16 @@
         keys, values = kall[u, :, 0:D], kall[u, :, D : 2 * D]
         sc[...] = dot(values, heads(dos[u]), 1, 1)
 
-        def blocks(b):
-            rows = pl.ds(pl.multiple_of(b * STEP, STEP), STEP)
-            return prob[u, rows, :].astype(F32), sc[rows, :]
-
-        def add(b, total):
-            p, dp_t = blocks(b)
-            return total + jnp.sum((p * dp_t).reshape(STEP // 8, 8, WIDE), axis=0)
-
-        total = lax.fori_loop(0, KEYS // STEP, add, jnp.zeros((8, WIDE), F32))
+        blocks = [slice(b, b + STEP) for b in range(0, KEYS, STEP)]
+        total = jnp.zeros((8, WIDE), F32)
+        for rows in blocks:
+            t = prob[u, rows, :].astype(F32) * sc[rows, :]
+            total = total + jnp.sum(t.reshape(STEP // 8, 8, WIDE), axis=0)
         inv = jnp.concatenate([invs[u, a : a + 1, :] for a in range(GR)], axis=1)
         delta = jnp.sum(total, axis=0, keepdims=True) * inv
 
-        def score(b, _):
-            p, dp_t = blocks(b)
-            dsb[pl.ds(pl.multiple_of(b * STEP, STEP), STEP), :] = (p * (dp_t - delta)).astype(BF)
-            return 0
-
-        lax.fori_loop(0, KEYS // STEP, score, 0)
+        for rows in blocks:
+            dsb[rows, :] = (prob[u, rows, :].astype(F32) * (sc[rows, :] - delta)).astype(BF)
         dq = dot(keys.T, dsb[...], 1, 0) * scale
         for a in range(GR):
             cols = slice(a * D, (a + 1) * D)

time: 61.9 us -> 59.9 us (0.968)
  Pallas kernels: 61 us -> 59.1 us
    pallas_call x1, Pallas kernels: 59.8 us -> 57.8 us  [body(): pl.pallas_call(kernel, out_shape=(vm((ROWS, WIDE), BF), vm((KV, D, WIDE),...]
where the time goes in v4:
time: 59.9 us; the launch traced here: 59.7 us
  Pallas kernels  59.1 us (99%)
  between operations  0.64 us (1%)
    pallas_call x1, Pallas kernels, body(): pl.pallas_call(kernel, out_shape=(vm((ROWS, WIDE), BF), vm((KV, D, WIDE),...  57.8 us
    pallas_call x1, Pallas kernels, body(): pl.pallas_call(finish, out_shape=(jax.ShapeDtypeStruct((D, KV * WIDE), BF...  1.24 us

profile of v4, /device:TPU:2, one launch (start us, length us, event | category | flops | bytes accessed | tf_op | source)
XLA Modules:
  0.0 59.7 jit_solution(7011744836680687562)
XLA Ops:
  0.6 57.8 %shard_map.102 = (bf16[512,640]{1,0:T(8,128)(2,1)S(1)}, bf16[4,128,640]{2,1,0:T(8,128)(2,1)S(1)}, bf16[4,128,256]{2,1,0:T(8,128)(2,1)S(1)}, bf16[4,128,256]{2,1,...) custom-call(bf16[128,2560]{1,0:T(8,128)(2,1)} %q_hbm.1, bf16[128,512]{1,0:T(8,128)(2,1)} %k_hbm.1, ...), custom_call_target="tpu_custom_call" | custom-call | tf_op jit(solution)/shard_map/pallas_call | solution.py:401
  58.5 1.2 %shard_map.103 = (bf16[128,2560]{1,0:T(8,128)(2,1)}, bf16[128,2560]{1,0:T(8,128)(2,1)}, bf16[128,512]{1,0:T(8,128)(2,1)}, bf16[128,512]{1,0:T(8,128)(2,1)}) custom-call(bf16[512,640]{1,0:T(8,128)(2,1)S(1)} %get-tuple-element.10.got, bf16[4,128,640]{2,1,0:T(8,128)(2,1)S(1)} %get-tuple-element.11.qg, bf16[4,128,256]{2,1,0:T(8,128)(2,1)S(1)} %get-tuple-element.12.grow, ...), custom_call_target="tpu_custom_call" | custom-call | tf_op jit(solution)/shard_map/pallas_call | solution.py:459

commit v5 on v4

--- a/solution.py
+++ b/solution.py
@@ -18,7 +18,6 @@
 WIDE = GR * D
 KEYS = 4 * D
 NEG = -1e30
-TURN = 13
 STEP = 32
 BF, F32 = jnp.bfloat16, jnp.float32
 
@@ -31,20 +30,23 @@
     return lax.broadcasted_iota(jnp.int32, shape, dim)
 
 
-def picks(c, ul):
-    return (ul == ((c >> 2) & 3) * D + (c >> 4) * 4 + (c & 3)).astype(BF)
-
-
-def scatter_matrix(orders):
-    pick = picks(iota((KV * D, ROWS), 1), iota((KV * D, ROWS), 0))
+def picks():
+    c, l = iota((ROWS, D), 0), iota((ROWS, D), 1)
+    entry = (l == (c >> 4) * 4 + (c & 3)).astype(F32)
+    device = (c >> 2) & 3
+    return jnp.concatenate(
+        [jnp.where(device == u, entry, 0.0).astype(BF) for u in range(KV)], axis=1
+    )
+
+
+def scatter_matrix(orders, pick):
     row, c = iota((D, ROWS), 0), iota((D, ROWS), 1)
-    target = dot(orders, pick, 1, 0) + (((c >> 2) & 3) * D).astype(F32)
+    target = dot(orders, pick, 1, 1) + (((c >> 2) & 3) * D).astype(F32)
     row = row.astype(F32)
     return jnp.concatenate([(target == row + float(t * D)).astype(BF) for t in range(KV)], axis=0)
 
 
-def gather_matrix(orders):
-    pick = picks(iota((ROWS, KV * D), 0), iota((ROWS, KV * D), 1))
+def gather_matrix(orders, pick):
     c, lane = iota((ROWS, D), 0), iota((ROWS, D), 1)
     target = dot(pick, orders, 1, 1) + (((c >> 2) & 3) * D).astype(F32)
     lane = lane.astype(F32)
@@ -60,7 +62,7 @@
     rcv2, qg, grow, gup, gdn, p_out,
     sizes, ffn_ref, att_ref, qb, kvb, qst, kvw, kall, prob, gin, snd1, rcv1, snd2,
     m_att, mt_att, ott, dos, sc, dsb, dqs, accw, gsend, bias, invs, flag,
-    in_sem, att_s, att_r, kv_s, kv_r, q_s, q_r, dq_s, dq_r, g_s, g_r,
+    in_sem, att_s, att_r, kv_s, kv_r, kz_s, kz_r, q_s, q_r, dq_s, dq_r, g_s, g_r,
     a1_s, a1_r, a2_s, a2_r,
 ):
     dp = lax.axis_index("dp")
@@ -133,35 +135,25 @@
     for i in (1, 2, 3):
         order_copy(i).start()
 
-    def kv_copy(i, what):
+    def kv_copy(i):
         g = (x + i) & 3
-        s = kv_s.at[i, what]
-        if what == 0:
-            return remote(kvb.at[g], kvw.at[4 + x], s, kv_r.at[4 + x], z * KV + g)
-        if what == 1:
-            return remote(kvb.at[g], kvw.at[8 + x], s, kv_r.at[8 + x], below + g)
-        return remote(kvb.at[g, 0:HALF], kvw.at[x, 0:HALF], s, kv_r.at[x], above + g)
-
-    def kv_all(action):
-        for i in (2, 1, 3):
-            action(kv_copy(i, 0))
-        for i in (2, 1, 3, 0):
-
-            @pl.when(x <= 2)
-            def _():
-                action(kv_copy(i, 1))
-
-            @pl.when(x >= 1)
-            def _():
-                action(kv_copy(i, 2))
-
-    kv_all(lambda c: c.start())
+        return remote(kvb.at[g], kvw.at[4 + x], kv_s.at[i], kv_r.at[x], z * KV + g)
+
+    def kv_arrived(i):
+        u = (x + i) & 3
+        remote(kvb.at[u], kvw.at[4 + u], kv_s.at[i], kv_r.at[u], z * KV + u).wait_recv()
+
+    kv_down = remote(kvw.at[4:7], kvw.at[8:11], kz_s.at[0], kz_r.at[0], below + x)
+    kv_up = remote(kvw.at[5:8, 0:HALF], kvw.at[1:4, 0:HALF], kz_s.at[1], kz_r.at[1], above + x)
+
+    for i in (2, 1, 3):
+        kv_copy(i).start()
 
     def q_copy(i):
         g = (x + i) & 3
         return remote(qb.at[g], qst.at[x], q_s.at[i], q_r.at[x], z * KV + g)
 
-    for i in (2, 1, 3):
+    for i in (1, 3):
         q_copy(i).start()
 
     def rows_at(i):
@@ -170,12 +162,18 @@
     def token_row(peer):
         return pl.ds(pl.multiple_of((peer & 3) * D + (peer >> 2) * CHUNK, CHUNK), CHUNK)
 
-    def send1(i, _):
-        peer = (me + TURN * i) & (N - 1)
-        remote(snd1.at[token_row(peer)], rcv1.at[rows_at(me)], a1_s, a1_r, peer).start()
-        return 0
-
-    lax.fori_loop(1, N, send1, 0)
+    def send_column(src, dst, src_at, dst_at, s, r, dx):
+        def one(i, _):
+            peer = ((z + (0x07162534 >> (4 * i))) & 7) * KV + ((x + dx) & 3)
+            remote(src.at[src_at(peer)], dst.at[dst_at(me)], s, r, peer).start()
+            return 0
+
+        lax.fori_loop(0, 8 if dx else 7, one, 0)
+
+    def send1(dx):
+        send_column(snd1, rcv1, token_row, rows_at, a1_s, a1_r, dx)
+
+    send1(0)
     rcv1[rows_at(me), :] = snd1[token_row(me), :]
 
     def whole(src, dst, s, r):
@@ -200,6 +198,13 @@
             bias[u, r * D : (r + 1) * D, :] = jnp.maximum(
                 jnp.where(qq >= HALF, later, NEG), jnp.where(kk < HALF, earlier, NEG)
             )
+    for i in (1, 3, 2):
+        kv_arrived(i)
+    kv_down.start()
+    kv_up.start()
+    q_copy(2).start()
+    for dx in (1, 3, 2):
+        send1(dx)
     accw[...] = jnp.zeros_like(accw)
     invs[...] = jnp.zeros_like(invs)
 
@@ -207,19 +212,15 @@
         order_arrived(i).wait_recv()
     orders = jnp.concatenate([att_ref[u] for u in range(KV)], axis=1)
     orders = jnp.broadcast_to(orders.astype(F32).astype(BF), (D, KV * D))
-    m_att[...] = scatter_matrix(orders)
-    mt_att[...] = gather_matrix(orders)
-
-    for e in range(1, 11):
-        rows = slice(0, HALF) if e < 4 else slice(0, D)
-        c = remote(kvb.at[0, rows], kvw.at[e, rows], kv_s.at[0, 0], kv_r.at[e], me ^ 1)
-        if 4 <= e < 8:
-            pl.when(x != e - 4)(c.wait_recv)
-        else:
-            c.wait_recv()
+    pick = picks()
+    m_att[...] = scatter_matrix(orders, pick)
+    mt_att[...] = gather_matrix(orders, pick)
+
+    kv_down.wait_recv()
+    kv_up.wait_recv()
 
     def forward(i, _):
-        u = (x + i) & 3
+        u = (x + (0xB4 >> (2 * i))) & 3
 
         @pl.when(i > 0)
         def _():
@@ -260,12 +261,8 @@
 
     snd2[...] = dot(mt_att[...], ott[...], 1, 1).astype(BF)
 
-    def send2(i, _):
-        peer = (me + TURN * i) & (N - 1)
-        remote(snd2.at[rows_at(peer)], rcv2.at[token_row(me)], a2_s, a2_r, peer).start()
-        return 0
-
-    lax.fori_loop(1, N, send2, 0)
+    for dx in (2, 1, 3, 0):
+        send_column(snd2, rcv2, rows_at, token_row, a2_s, a2_r, dx)
     rcv2[token_row(me), :] = snd2[rows_at(me), :]
 
     whole(snd1, rcv1, a1_s, a1_r).wait_recv()
@@ -346,8 +343,10 @@
 
     for i in (1, 2, 3):
         order_copy(i).wait_send()
+        kv_copy(i).wait_send()
         q_copy(i).wait_send()
-    kv_all(lambda c: c.wait_send())
+    kv_down.wait_send()
+    kv_up.wait_send()
     whole(snd1, rcv1, a1_s, a1_r).wait_send()
     whole(snd2, rcv2, a2_s, a2_r).wait_send()
     for e in (8, 9, 10, 1, 2, 3):
@@ -439,8 +438,10 @@
             dma((16,)),
             dma((4,)),
             dma((4,)),
-            dma((4, 3)),
-            dma((12,)),
+            dma((4,)),
+            dma((4,)),
+            dma((2,)),
+            dma((2,)),
             dma((4,)),
             dma((4,)),
             dma((4,)),

time: 59.9 us -> 53.9 us (0.90)
  Pallas kernels: 59.1 us -> 53.1 us
    pallas_call x1, Pallas kernels: 57.8 us -> 51.9 us  [body(): pl.pallas_call(kernel, out_shape=(vm((ROWS, WIDE), BF), vm((KV, D, WIDE),...]
where the time goes in v5:
time: 53.9 us; the launch traced here: 53.7 us
  Pallas kernels  53.1 us (99%)
  between operations  0.64 us (1%)
    pallas_call x1, Pallas kernels, body(): pl.pallas_call(kernel, out_shape=(vm((ROWS, WIDE), BF), vm((KV, D, WIDE),...  51.9 us
    pallas_call x1, Pallas kernels, body(): pl.pallas_call(finish, out_shape=(jax.ShapeDtypeStruct((D, KV * WIDE), BF...  1.24 us

profile of v5, /device:TPU:2, one launch (start us, length us, event | category | flops | bytes accessed | tf_op | source)
XLA Modules:
  0.0 53.7 jit_solution(2389880245053205232)
XLA Ops:
  0.6 51.9 %shard_map.102 = (bf16[512,640]{1,0:T(8,128)(2,1)S(1)}, bf16[4,128,640]{2,1,0:T(8,128)(2,1)S(1)}, bf16[4,128,256]{2,1,0:T(8,128)(2,1)S(1)}, bf16[4,128,256]{2,1,...) custom-call(bf16[128,2560]{1,0:T(8,128)(2,1)} %q_hbm.1, bf16[128,512]{1,0:T(8,128)(2,1)} %k_hbm.1, ...), custom_call_target="tpu_custom_call" | custom-call | tf_op jit(solution)/shard_map/pallas_call | solution.py:400
  52.5 1.2 %shard_map.103 = (bf16[128,2560]{1,0:T(8,128)(2,1)}, bf16[128,2560]{1,0:T(8,128)(2,1)}, bf16[128,512]{1,0:T(8,128)(2,1)}, bf16[128,512]{1,0:T(8,128)(2,1)}) custom-call(bf16[512,640]{1,0:T(8,128)(2,1)S(1)} %get-tuple-element.10.got, bf16[4,128,640]{2,1,0:T(8,128)(2,1)S(1)} %get-tuple-element.11.qg, bf16[4,128,256]{2,1,0:T(8,128)(2,1)S(1)} %get-tuple-element.12.grow, ...), custom_call_target="tpu_custom_call" | custom-call | tf_op jit(solution)/shard_map/pallas_call | solution.py:460

commit v6 on v5

--- a/solution.py
+++ b/solution.py
@@ -62,7 +62,7 @@
     rcv2, qg, grow, gup, gdn, p_out,
     sizes, ffn_ref, att_ref, qb, kvb, qst, kvw, kall, prob, gin, snd1, rcv1, snd2,
     m_att, mt_att, ott, dos, sc, dsb, dqs, accw, gsend, bias, invs, flag,
-    in_sem, att_s, att_r, kv_s, kv_r, kz_s, kz_r, q_s, q_r, dq_s, dq_r, g_s, g_r,
+    in_sem, att_s, att_r, kv_s, kv_r, kz_s, kz_r, f_s, f_r, q_s, q_r, dq_s, dq_r, g_s, g_r,
     a1_s, a1_r, a2_s, a2_r,
 ):
     dp = lax.axis_index("dp")
@@ -108,6 +108,51 @@
     for c in local[4:] + local[:4]:
         c.start()
 
+    for c in local[2:]:
+        c.wait()
+    kvw[4 + x] = kvb[x]
+    qst[x] = qb[x]
+
+    pl.semaphore_wait(barrier, N - 1)
+
+    def order_copy(i):
+        return remote(att_ref.at[x], att_ref.at[x], att_s.at[i], att_r.at[i], z * KV + ((x + i) & 3))
+
+    def order_arrived(i):
+        u = (x + 4 - i) & 3
+        return remote(att_ref.at[u], att_ref.at[u], att_s.at[i], att_r.at[i], me ^ 1)
+
+    for i in (1, 2, 3):
+        order_copy(i).start()
+
+    def kv_copy(i):
+        g = (x + i) & 3
+        return remote(kvb.at[g], kvw.at[4 + x], kv_s.at[i], kv_r.at[x], z * KV + g)
+
+    def kv_arrived(i):
+        u = (x + i) & 3
+        remote(kvb.at[u], kvw.at[4 + u], kv_s.at[i], kv_r.at[u], z * KV + u).wait_recv()
+
+    kv_down = remote(kvw.at[4:7], kvw.at[8:11], kz_s.at[0], kz_r.at[0], below + x)
+    kv_up = remote(kvw.at[5:8, 0:HALF], kvw.at[1:4, 0:HALF], kz_s.at[1], kz_r.at[1], above + x)
+
+    for i in (2, 1, 3):
+        kv_copy(i).start()
+
+    def q_copy(i):
+        g = (x + i) & 3
+        return remote(qb.at[g], qst.at[x], q_s.at[i], q_r.at[x], z * KV + g)
+
+    QUARTER = D // 4
+
+    def far_copy(k):
+        rows = slice(k * QUARTER, (k + 1) * QUARTER)
+        g = x ^ 2
+        return remote(qb.at[g, rows], qst.at[x, rows], f_s.at[k], f_r.at[k], z * KV + g)
+
+    for i in (1, 3):
+        q_copy(i).start()
+
     local[0].wait()
     order = ffn_ref[...].astype(F32)
     p_ffn = (order == iota((D, D), 0).astype(F32)).astype(BF)
@@ -117,44 +162,6 @@
     packed = dot(gather_ffn, gin[...], 1, 0).astype(BF)
     for g in range(KV):
         snd1[g * D : (g + 1) * D, :] = packed[:, g * WIDE : (g + 1) * WIDE]
-
-    for c in local[2:]:
-        c.wait()
-    kvw[4 + x] = kvb[x]
-    qst[x] = qb[x]
-
-    pl.semaphore_wait(barrier, N - 1)
-
-    def order_copy(i):
-        return remote(att_ref.at[x], att_ref.at[x], att_s.at[i], att_r.at[i], z * KV + ((x + i) & 3))
-
-    def order_arrived(i):
-        u = (x + 4 - i) & 3
-        return remote(att_ref.at[u], att_ref.at[u], att_s.at[i], att_r.at[i], me ^ 1)
-
-    for i in (1, 2, 3):
-        order_copy(i).start()
-
-    def kv_copy(i):
-        g = (x + i) & 3
-        return remote(kvb.at[g], kvw.at[4 + x], kv_s.at[i], kv_r.at[x], z * KV + g)
-
-    def kv_arrived(i):
-        u = (x + i) & 3
-        remote(kvb.at[u], kvw.at[4 + u], kv_s.at[i], kv_r.at[u], z * KV + u).wait_recv()
-
-    kv_down = remote(kvw.at[4:7], kvw.at[8:11], kz_s.at[0], kz_r.at[0], below + x)
-    kv_up = remote(kvw.at[5:8, 0:HALF], kvw.at[1:4, 0:HALF], kz_s.at[1], kz_r.at[1], above + x)
-
-    for i in (2, 1, 3):
-        kv_copy(i).start()
-
-    def q_copy(i):
-        g = (x + i) & 3
-        return remote(qb.at[g], qst.at[x], q_s.at[i], q_r.at[x], z * KV + g)
-
-    for i in (1, 3):
-        q_copy(i).start()
 
     def rows_at(i):
         return pl.ds(pl.multiple_of(i * CHUNK, CHUNK), CHUNK)
@@ -202,7 +209,8 @@
         kv_arrived(i)
     kv_down.start()
     kv_up.start()
-    q_copy(2).start()
+    for k in range(4):
+        far_copy(k).start()
     for dx in (1, 3, 2):
         send1(dx)
     accw[...] = jnp.zeros_like(accw)
@@ -222,9 +230,14 @@
     def forward(i, _):
         u = (x + (0xB4 >> (2 * i))) & 3
 
-        @pl.when(i > 0)
+        @pl.when((i == 1) | (i == 2))
         def _():
             remote(qb.at[0], qst.at[u], q_s.at[0], q_r.at[u], me ^ 1).wait_recv()
+
+        @pl.when(i == 3)
+        def _():
+            for k in range(4):
+                far_copy(k).wait_recv()
 
         kall[u, 0:D, :] = kvw[4 + u]
         for r in (1, 2, 3):
@@ -277,6 +290,43 @@
     def dq_copy(u):
         return remote(dqs.at[u], qg.at[x], dq_s.at[u], dq_r.at[x], z * KV + u)
 
+    def add_part(part, u, term):
+        accw[part, 4 + u] += term[0:D]
+        for r in (1, 2, 3):
+            later = flag[u * KV + r] > 0
+            accw[part, 4 + u + r] += jnp.where(later, term[r * D : (r + 1) * D], 0.0)
+            accw[part, u + r, 0:HALF, :] += jnp.where(later, 0.0, term[r * D : r * D + HALF])
+
+    def g_copy(part, e):
+        g, s = e & 3, g_s.at[part, e]
+        if e < 4:
+            return remote(gsend.at[part, e, 0:HALF], gdn.at[x, part], s, g_r.at[0, part, x], below + g)
+        if e < 8:
+            return remote(gsend.at[part, e], grow.at[x, part], s, g_r.at[1, part, x], z * KV + g)
+        return remote(gsend.at[part, e], gup.at[x, part], s, g_r.at[2, part, x], above + g)
+
+    def g_all(part, action):
+        for e in (8, 9, 10, 1, 2, 3):
+            action(g_copy(part, e))
+        for e in range(4, 8):
+
+            @pl.when(x != e - 4)
+            def _():
+                action(g_copy(part, e))
+
+    def send_terms(part):
+        for e in range(1, 11):
+            gsend[part, e] = accw[part, e].astype(BF)
+        g_all(part, lambda c: c.start())
+        grow[x, part] = gsend[part, 4 + x]
+
+    def value_terms(u, _):
+        add_part(1, u, dot(prob[u], heads(dos[u]), 1, 0))
+        return 0
+
+    lax.fori_loop(0, KV, value_terms, 0)
+    send_terms(1)
+
     def backward(i, _):
         u = (x + 1 + i) & 3
         keys, values = kall[u, :, 0:D], kall[u, :, D : 2 * D]
@@ -301,61 +351,50 @@
         def _():
             dq_copy(u).start()
 
-        kpart = dot(dsb[...], heads(qst[u]), 1, 0) * scale
-        vpart = dot(prob[u], heads(dos[u]), 1, 0)
-        part = jnp.concatenate([kpart, vpart], axis=1)
-        accw[4 + u] += part[0:D]
-        for r in (1, 2, 3):
-            later = flag[u * KV + r] > 0
-            accw[4 + u + r] += jnp.where(later, part[r * D : (r + 1) * D], 0.0)
-            accw[u + r, 0:HALF, :] += jnp.where(later, 0.0, part[r * D : r * D + HALF])
+        add_part(0, u, dot(dsb[...], heads(qst[u]), 1, 0) * scale)
         return 0
 
     lax.fori_loop(0, KV, backward, 0)
     qg[x] = dqs[x]
 
-    for e in range(1, 11):
-        gsend[e] = accw[e].astype(BF)
-
-    def g_copy(e):
-        g = e & 3
-        if e < 4:
-            return remote(gsend.at[e, 0:HALF], gdn.at[x], g_s.at[e], g_r.at[0, x], below + g)
-        if e < 8:
-            return remote(gsend.at[e], grow.at[x], g_s.at[e], g_r.at[1, x], z * KV + g)
-        return remote(gsend.at[e], gup.at[x], g_s.at[e], g_r.at[2, x], above + g)
-
-    for e in (8, 9, 10, 1, 2, 3):
-        g_copy(e).start()
-    for e in range(4, 8):
-        pl.when(x != e - 4)(g_copy(e).start)
-    grow[x] = gsend[4 + x]
+    send_terms(0)
 
     whole(snd2, rcv2, a2_s, a2_r).wait_recv()
-    for g in range(KV):
-        pl.when(x != g)(
-            remote(gsend.at[4], grow.at[g], g_s.at[0], g_r.at[1, g], me ^ 1).wait_recv
-        )
-        pl.when(x <= 2)(remote(gsend.at[4], gup.at[g], g_s.at[0], g_r.at[2, g], me ^ 1).wait_recv)
-        pl.when(x >= 1)(
-            remote(gsend.at[4, 0:HALF], gdn.at[g], g_s.at[0], g_r.at[0, g], me ^ 1).wait_recv
-        )
+    for part in (1, 0):
+        for g in range(KV):
+            pl.when(x != g)(
+                remote(
+                    gsend.at[0, 4], grow.at[g, part], g_s.at[0, 0], g_r.at[1, part, g], me ^ 1
+                ).wait_recv
+            )
+            pl.when(x <= 2)(
+                remote(
+                    gsend.at[0, 4], gup.at[g, part], g_s.at[0, 0], g_r.at[2, part, g], me ^ 1
+                ).wait_recv
+            )
+            pl.when(x >= 1)(
+                remote(
+                    gsend.at[0, 4, 0:HALF], gdn.at[g, part], g_s.at[0, 0], g_r.at[0, part, g], me ^ 1
+                ).wait_recv
+            )
 
     for i in (1, 2, 3):
         order_copy(i).wait_send()
         kv_copy(i).wait_send()
+    for i in (1, 3):
         q_copy(i).wait_send()
+    for k in range(4):
+        far_copy(k).wait_send()
     kv_down.wait_send()
     kv_up.wait_send()
     whole(snd1, rcv1, a1_s, a1_r).wait_send()
     whole(snd2, rcv2, a2_s, a2_r).wait_send()
-    for e in (8, 9, 10, 1, 2, 3):
-        g_copy(e).wait_send()
+    for part in (0, 1):
+        g_all(part, lambda c: c.wait_send())
     for u in range(KV):
 
         @pl.when(x != u)
         def _():
-            g_copy(4 + u).wait_send()
             dq_copy(u).wait_send()
             remote(dqs.at[u], qg.at[u], dq_s.at[u], dq_r.at[u], me ^ 1).wait_recv()
 
@@ -375,13 +414,12 @@
     for g in range(KV):
         send(qg.at[g], qg_hbm.at[:, g * WIDE : (g + 1) * WIDE])
     for g in range(KV):
-        total = grow[g].astype(F32) + jnp.where(x <= 2, gup[g].astype(F32), 0.0)
-        low = total[0:HALF] + jnp.where(x >= 1, gdn[g].astype(F32), 0.0)
-        high = total[HALF:D]
         cols = slice(g * D, (g + 1) * D)
-        for ref, lane in ((kg_v, 0), (vg_v, D)):
-            ref[0:HALF, cols] = low[:, lane : lane + D].astype(BF)
-            ref[HALF:D, cols] = high[:, lane : lane + D].astype(BF)
+        for part, ref in ((0, kg_v), (1, vg_v)):
+            total = grow[g, part].astype(F32) + jnp.where(x <= 2, gup[g, part].astype(F32), 0.0)
+            low = total[0:HALF] + jnp.where(x >= 1, gdn[g, part].astype(F32), 0.0)
+            ref[0:HALF, cols] = low.astype(BF)
+            ref[HALF:D, cols] = total[HALF:D].astype(BF)
     send(kg_v, kg_hbm)
     send(vg_v, vg_hbm)
     for g in range(KV):
@@ -402,9 +440,9 @@
         out_shape=(
             vm((ROWS, WIDE), BF),
             vm((KV, D, WIDE), BF),
-            vm((KV, D, 2 * D), BF),
-            vm((KV, D, 2 * D), BF),
-            vm((KV, HALF, 2 * D), BF),
+            vm((KV, 2, D, D), BF),
+            vm((KV, 2, D, D), BF),
+            vm((KV, 2, HALF, D), BF),
             vm((D, D), BF),
         ),
         in_specs=[hbm] * 7,
@@ -430,8 +468,8 @@
             vm((KEYS, WIDE), F32),
             vm((KEYS, WIDE), BF),
             vm((KV, D, WIDE), BF),
-            vm((12, D, 2 * D), F32),
-            vm((12, D, 2 * D), BF),
+            vm((2, 12, D, D), F32),
+            vm((2, 12, D, D), BF),
             vm((KV, KEYS, D), F32),
             vm((KV, 8, D), F32),
             pltpu.SMEM((KV * KV,), jnp.int32),
@@ -446,8 +484,10 @@
             dma((4,)),
             dma((4,)),
             dma((4,)),
-            dma((12,)),
-            dma((3, 4)),
+            dma((4,)),
+            dma((4,)),
+            dma((2, 12)),
+            dma((3, 2, 4)),
             dma,
             dma,
             dma,

time: 53.9 us -> 54.3 us (level)
  no operation moved by 1% of the time
where the time goes in v6:
time: 54.3 us; the launch traced here: 54.2 us
  Pallas kernels  53.6 us (99%)
  between operations  0.64 us (1%)
    pallas_call x1, Pallas kernels, body(): pl.pallas_call(kernel, out_shape=(vm((ROWS, WIDE), BF), vm((KV, D, WIDE),...  52.3 us
    pallas_call x1, Pallas kernels, body(): pl.pallas_call(finish, out_shape=(jax.ShapeDtypeStruct((D, KV * WIDE), BF...  1.24 us

profile of v6, /device:TPU:2, one launch (start us, length us, event | category | flops | bytes accessed | tf_op | source)
XLA Modules:
  0.0 54.2 jit_solution(13023200266601993643)
XLA Ops:
  0.6 52.3 %shard_map.102 = (bf16[512,640]{1,0:T(8,128)(2,1)S(1)}, bf16[4,128,640]{2,1,0:T(8,128)(2,1)S(1)}, bf16[4,2,128,128]{3,2,1,0:T(8,128)(2,1)S(1)}, bf16[4,2,128,128...) custom-call(bf16[128,2560]{1,0:T(8,128)(2,1)} %q_hbm.1, ...), custom_call_target="tpu_custom_call" | custom-call | tf_op jit(solution)/shard_map/pallas_call | solution.py:438
  53.0 1.2 %shard_map.103 = (bf16[128,2560]{1,0:T(8,128)(2,1)}, bf16[128,2560]{1,0:T(8,128)(2,1)}, bf16[128,512]{1,0:T(8,128)(2,1)}, bf16[128,512]{1,0:T(8,128)(2,1)}) custom-call(bf16[512,640]{1,0:T(8,128)(2,1)S(1)} %get-tuple-element.10.got, bf16[4,128,640]{2,1,0:T(8,128)(2,1)S(1)} %get-tuple-element.11.qg, bf16[4,2,128,128]{3,2,1,0:T(8,128)(2,1)S(1)} %get-tuple-element.12.grow, ...), custom_call_target="tpu_custom_call" | custom-call | tf_op jit(solution)/shard_map/pallas_call | solution.py:500

commit v7 on v6

--- a/solution.py
+++ b/solution.py
@@ -211,8 +211,6 @@
     kv_up.start()
     for k in range(4):
         far_copy(k).start()
-    for dx in (1, 3, 2):
-        send1(dx)
     accw[...] = jnp.zeros_like(accw)
     invs[...] = jnp.zeros_like(invs)
 
@@ -226,6 +224,8 @@
 
     kv_down.wait_recv()
     kv_up.wait_recv()
+    for dx in (1, 3, 2):
+        send1(dx)
 
     def forward(i, _):
         u = (x + (0xB4 >> (2 * i))) & 3

time: 54.3 us -> 56.5 us (1.041)
  Pallas kernels: 53.6 us -> 55.7 us
    pallas_call x1, Pallas kernels: 52.3 us -> 54.5 us  [body(): pl.pallas_call(kernel, out_shape=(vm((ROWS, WIDE), BF), vm((KV, D, WIDE),...]
where the time goes in v7:
time: 56.5 us; the launch traced here: 56.3 us
  Pallas kernels  55.7 us (99%)
  between operations  0.64 us (1%)
    pallas_call x1, Pallas kernels, body(): pl.pallas_call(kernel, out_shape=(vm((ROWS, WIDE), BF), vm((KV, D, WIDE),...  54.5 us
    pallas_call x1, Pallas kernels, body(): pl.pallas_call(finish, out_shape=(jax.ShapeDtypeStruct((D, KV * WIDE), BF...  1.24 us

profile of v7, /device:TPU:2, one launch (start us, length us, event | category | flops | bytes accessed | tf_op | source)
XLA Modules:
  0.0 56.3 jit_solution(14986021122600331052)
XLA Ops:
  0.6 54.5 %shard_map.102 = (bf16[512,640]{1,0:T(8,128)(2,1)S(1)}, bf16[4,128,640]{2,1,0:T(8,128)(2,1)S(1)}, bf16[4,2,128,128]{3,2,1,0:T(8,128)(2,1)S(1)}, bf16[4,2,128,128...) custom-call(bf16[128,2560]{1,0:T(8,128)(2,1)} %q_hbm.1, ...), custom_call_target="tpu_custom_call" | custom-call | tf_op jit(solution)/shard_map/pallas_call | solution.py:438
  55.1 1.2 %shard_map.103 = (bf16[128,2560]{1,0:T(8,128)(2,1)}, bf16[128,2560]{1,0:T(8,128)(2,1)}, bf16[128,512]{1,0:T(8,128)(2,1)}, bf16[128,512]{1,0:T(8,128)(2,1)}) custom-call(bf16[512,640]{1,0:T(8,128)(2,1)S(1)} %get-tuple-element.10.got, bf16[4,128,640]{2,1,0:T(8,128)(2,1)S(1)} %get-tuple-element.11.qg, bf16[4,2,128,128]{3,2,1,0:T(8,128)(2,1)S(1)} %get-tuple-element.12.grow, ...), custom_call_target="tpu_custom_call" | custom-call | tf_op jit(solution)/shard_map/pallas_call | solution.py:500

commit v8 on v5

--- a/solution.py
+++ b/solution.py
@@ -61,7 +61,7 @@
     q_hbm, k_hbm, v_hbm, g_hbm, sizes_hbm, ffn_hbm, att_hbm,
     rcv2, qg, grow, gup, gdn, p_out,
     sizes, ffn_ref, att_ref, qb, kvb, qst, kvw, kall, prob, gin, snd1, rcv1, snd2,
-    m_att, mt_att, ott, dos, sc, dsb, dqs, accw, gsend, bias, invs, flag,
+    m_att, mt_att, ott, dos, sc0, sc1, dsb0, dsb1, dqs, accw, gsend, bias, invs, flag,
     in_sem, att_s, att_r, kv_s, kv_r, kz_s, kz_r, q_s, q_r, dq_s, dq_r, g_s, g_r,
     a1_s, a1_r, a2_s, a2_r,
 ):
@@ -70,6 +70,7 @@
     z, x = me >> 2, me & 3
     above, below = ((z + 1) & 7) * KV, ((z + 7) & 7) * KV
     scale = 1.0 / math.sqrt(D)
+    sc, dsb = (sc0, sc1), (dsb0, dsb1)
 
     def remote(src, dst, s, r, peer):
         return pltpu.make_async_remote_copy(
@@ -219,45 +220,56 @@
     kv_down.wait_recv()
     kv_up.wait_recv()
 
-    def forward(i, _):
-        u = (x + (0xB4 >> (2 * i))) & 3
-
-        @pl.when(i > 0)
-        def _():
-            remote(qb.at[0], qst.at[u], q_s.at[0], q_r.at[u], me ^ 1).wait_recv()
-
-        kall[u, 0:D, :] = kvw[4 + u]
+    order_u = [(x + dx) & 3 for dx in (0, 1, 3, 2)]
+    halves = [slice(b, b + STEP) for b in range(0, KEYS, STEP)]
+
+    def scores(i):
+        u = order_u[i]
+        kall[i, 0:D, :] = kvw[4 + u]
         for r in (1, 2, 3):
-            kall[u, r * D : r * D + HALF, :] = jnp.where(
+            kall[i, r * D : r * D + HALF, :] = jnp.where(
                 flag[u * KV + r] > 0, kvw[4 + u + r, 0:HALF, :], kvw[u + r, 0:HALF, :]
             )
-            kall[u, r * D + HALF : (r + 1) * D, :] = kvw[4 + u + r, HALF:D, :]
-        keys, values = kall[u, :, 0:D], kall[u, :, D : 2 * D]
-        sc[...] = dot(keys, heads(qst[u]), 1, 1)
-
-        blocks = [slice(b, b + STEP) for b in range(0, KEYS, STEP)]
+            kall[i, r * D + HALF : (r + 1) * D, :] = kvw[4 + u + r, HALF:D, :]
+        sc[i % 2][...] = dot(kall[i, :, 0:D], heads(qst[u]), 1, 1)
+
+    def soften(i):
+        u = order_u[i]
 
         def masked(rows):
-            return sc[rows, :] + jnp.concatenate([bias[u, rows, :]] * GR, axis=1)
+            return sc[i % 2][rows, :] + jnp.concatenate([bias[u, rows, :]] * GR, axis=1)
 
         top = jnp.full((8, WIDE), NEG, F32)
-        for rows in blocks:
+        for rows in halves:
             top = jnp.maximum(top, jnp.max(masked(rows).reshape(STEP // 8, 8, WIDE), axis=0))
         top = jnp.max(top, axis=0, keepdims=True)
         total = jnp.zeros((8, WIDE), F32)
-        for rows in blocks:
+        for rows in halves:
             p = jnp.exp2((masked(rows) - top) * (scale * math.log2(math.e)))
-            prob[u, rows, :] = p.astype(BF)
+            prob[i, rows, :] = p.astype(BF)
             total = total + jnp.sum(p.reshape(STEP // 8, 8, WIDE), axis=0)
         inv = 1.0 / jnp.sum(total, axis=0, keepdims=True)
-        o = (dot(values.T, prob[u], 1, 0) * inv).astype(BF)
+        o = (dot(kall[i, :, D : 2 * D].T, prob[i], 1, 0) * inv).astype(BF)
         for a in range(GR):
             cols = slice(a * D, (a + 1) * D)
             ott[cols, lanes(u, D)] = o[:, cols]
-            invs[u, a : a + 1, :] = inv[:, cols]
-        return 0
-
-    lax.fori_loop(0, KV, forward, 0)
+            invs[i, a : a + 1, :] = inv[:, cols]
+
+    def q_arrived(i):
+        u = order_u[i]
+        remote(qb.at[0], qst.at[u], q_s.at[0], q_r.at[u], me ^ 1).wait_recv()
+
+    scores(0)
+    soften(0)
+    q_arrived(1)
+    scores(1)
+    q_arrived(2)
+    scores(2)
+    soften(1)
+    q_arrived(3)
+    scores(3)
+    soften(2)
+    soften(3)
 
     snd2[...] = dot(mt_att[...], ott[...], 1, 1).astype(BF)
 
@@ -269,7 +281,7 @@
     every = dot(m_att[...], rcv1[...], 1, 0)
     for u in range(KV):
         up = every[u * D : (u + 1) * D]
-        inv = invs[u].T
+        inv = invs[(0xB4 >> (2 * ((u - x) & 3))) & 3].T
         for a in range(GR):
             cols = slice(a * D, (a + 1) * D)
             dos[u, :, cols] = (up[:, cols] * inv[:, a : a + 1]).astype(BF)
@@ -277,41 +289,47 @@
     def dq_copy(u):
         return remote(dqs.at[u], qg.at[x], dq_s.at[u], dq_r.at[x], z * KV + u)
 
-    def backward(i, _):
-        u = (x + 1 + i) & 3
-        keys, values = kall[u, :, 0:D], kall[u, :, D : 2 * D]
-        sc[...] = dot(values, heads(dos[u]), 1, 1)
-
-        blocks = [slice(b, b + STEP) for b in range(0, KEYS, STEP)]
+    def up_scores(i):
+        sc[i % 2][...] = dot(kall[i, :, D : 2 * D], heads(dos[order_u[i]]), 1, 1)
+
+    def slopes(i):
         total = jnp.zeros((8, WIDE), F32)
-        for rows in blocks:
-            t = prob[u, rows, :].astype(F32) * sc[rows, :]
+        for rows in halves:
+            t = prob[i, rows, :].astype(F32) * sc[i % 2][rows, :]
             total = total + jnp.sum(t.reshape(STEP // 8, 8, WIDE), axis=0)
-        inv = jnp.concatenate([invs[u, a : a + 1, :] for a in range(GR)], axis=1)
+        inv = jnp.concatenate([invs[i, a : a + 1, :] for a in range(GR)], axis=1)
         delta = jnp.sum(total, axis=0, keepdims=True) * inv
-
-        for rows in blocks:
-            dsb[rows, :] = (prob[u, rows, :].astype(F32) * (sc[rows, :] - delta)).astype(BF)
-        dq = dot(keys.T, dsb[...], 1, 0) * scale
+        for rows in halves:
+            dsb[i % 2][rows, :] = (
+                prob[i, rows, :].astype(F32) * (sc[i % 2][rows, :] - delta)
+            ).astype(BF)
+
+    def gradients(i):
+        u = order_u[i]
+        ds = dsb[i % 2][...]
+        dq = (dot(kall[i, :, 0:D].T, ds, 1, 0) * scale).astype(BF)
         for a in range(GR):
             cols = slice(a * D, (a + 1) * D)
-            dqs[u, :, cols] = dq[:, cols].T.astype(BF)
-
-        @pl.when(i < 3)
-        def _():
-            dq_copy(u).start()
-
-        kpart = dot(dsb[...], heads(qst[u]), 1, 0) * scale
-        vpart = dot(prob[u], heads(dos[u]), 1, 0)
+            dqs[u, :, cols] = dq[:, cols].T
+        kpart = dot(ds, heads(qst[u]), 1, 0) * scale
+        vpart = dot(prob[i], heads(dos[u]), 1, 0)
         part = jnp.concatenate([kpart, vpart], axis=1)
         accw[4 + u] += part[0:D]
         for r in (1, 2, 3):
             later = flag[u * KV + r] > 0
             accw[4 + u + r] += jnp.where(later, part[r * D : (r + 1) * D], 0.0)
             accw[u + r, 0:HALF, :] += jnp.where(later, 0.0, part[r * D : r * D + HALF])
-        return 0
-
-    lax.fori_loop(0, KV, backward, 0)
+
+    up_scores(3)
+    up_scores(2)
+    slopes(3)
+    for i in (3, 2, 1):
+        gradients(i)
+        if i > 1:
+            up_scores(i - 2)
+        slopes(i - 1)
+        dq_copy(order_u[i]).start()
+    gradients(0)
     qg[x] = dqs[x]
 
     for e in range(1, 11):
@@ -428,6 +446,8 @@
             vm((WIDE, KV * D), BF),
             vm((KV, D, WIDE), BF),
             vm((KEYS, WIDE), F32),
+            vm((KEYS, WIDE), F32),
+            vm((KEYS, WIDE), BF),
             vm((KEYS, WIDE), BF),
             vm((KV, D, WIDE), BF),
             vm((12, D, 2 * D), F32),

time: 53.9 us -> 53.8 us (level)
  no operation moved by 1% of the time
where the time goes in v8:
time: 53.8 us; the launch traced here: 53.7 us
  Pallas kernels  53.1 us (99%)
  between operations  0.64 us (1%)
    pallas_call x1, Pallas kernels, body(): pl.pallas_call(kernel, out_shape=(vm((ROWS, WIDE), BF), vm((KV, D, WIDE),...  51.8 us
    pallas_call x1, Pallas kernels, body(): pl.pallas_call(finish, out_shape=(jax.ShapeDtypeStruct((D, KV * WIDE), BF...  1.24 us

profile of v8, /device:TPU:2, one launch (start us, length us, event | category | flops | bytes accessed | tf_op | source)
XLA Modules:
  0.0 53.7 jit_solution(15328347972697171772)
XLA Ops:
  0.6 51.8 %shard_map.102 = (bf16[512,640]{1,0:T(8,128)(2,1)S(1)}, bf16[4,128,640]{2,1,0:T(8,128)(2,1)S(1)}, bf16[4,128,256]{2,1,0:T(8,128)(2,1)S(1)}, bf16[4,128,256]{2,1,...) custom-call(bf16[128,2560]{1,0:T(8,128)(2,1)} %q_hbm.1, bf16[128,512]{1,0:T(8,128)(2,1)} %k_hbm.1, ...), custom_call_target="tpu_custom_call" | custom-call | tf_op jit(solution)/shard_map/pallas_call | solution.py:418
  52.5 1.2 %shard_map.103 = (bf16[128,2560]{1,0:T(8,128)(2,1)}, bf16[128,2560]{1,0:T(8,128)(2,1)}, bf16[128,512]{1,0:T(8,128)(2,1)}, bf16[128,512]{1,0:T(8,128)(2,1)}) custom-call(bf16[512,640]{1,0:T(8,128)(2,1)S(1)} %get-tuple-element.10.got, bf16[4,128,640]{2,1,0:T(8,128)(2,1)S(1)} %get-tuple-element.11.qg, bf16[4,128,256]{2,1,0:T(8,128)(2,1)S(1)} %get-tuple-element.12.grow, ...), custom_call_target="tpu_custom_call" | custom-call | tf_op jit(solution)/shard_map/pallas_call | solution.py:480

commit v9 on v5

--- a/solution.py
+++ b/solution.py
@@ -143,8 +143,25 @@
         u = (x + i) & 3
         remote(kvb.at[u], kvw.at[4 + u], kv_s.at[i], kv_r.at[u], z * KV + u).wait_recv()
 
-    kv_down = remote(kvw.at[4:7], kvw.at[8:11], kz_s.at[0], kz_r.at[0], below + x)
-    kv_up = remote(kvw.at[5:8, 0:HALF], kvw.at[1:4, 0:HALF], kz_s.at[1], kz_r.at[1], above + x)
+    def kv_pieces(action):
+        for k in range(D // STEP):
+            rows = slice(k * STEP, (k + 1) * STEP)
+            for e in (4, 5, 6):
+                action(
+                    remote(
+                        kvw.at[e, rows], kvw.at[e + 4, rows], kz_s.at[0, e - 4, k],
+                        kz_r.at[0, e - 4, k], below + x,
+                    )
+                )
+            if k >= HALF // STEP:
+                continue
+            for e in (5, 6, 7):
+                action(
+                    remote(
+                        kvw.at[e, rows], kvw.at[e - 4, rows], kz_s.at[1, e - 5, k],
+                        kz_r.at[1, e - 5, k], above + x,
+                    )
+                )
 
     for i in (2, 1, 3):
         kv_copy(i).start()
@@ -173,7 +190,8 @@
     def send1(dx):
         send_column(snd1, rcv1, token_row, rows_at, a1_s, a1_r, dx)
 
-    send1(0)
+    for dx in (0, 1, 3, 2):
+        send1(dx)
     rcv1[rows_at(me), :] = snd1[token_row(me), :]
 
     def whole(src, dst, s, r):
@@ -200,11 +218,8 @@
             )
     for i in (1, 3, 2):
         kv_arrived(i)
-    kv_down.start()
-    kv_up.start()
+    kv_pieces(lambda c: c.start())
     q_copy(2).start()
-    for dx in (1, 3, 2):
-        send1(dx)
     accw[...] = jnp.zeros_like(accw)
     invs[...] = jnp.zeros_like(invs)
 
@@ -216,8 +231,7 @@
     m_att[...] = scatter_matrix(orders, pick)
     mt_att[...] = gather_matrix(orders, pick)
 
-    kv_down.wait_recv()
-    kv_up.wait_recv()
+    kv_pieces(lambda c: c.wait_recv())
 
     def forward(i, _):
         u = (x + (0xB4 >> (2 * i))) & 3
@@ -345,8 +359,7 @@
         order_copy(i).wait_send()
         kv_copy(i).wait_send()
         q_copy(i).wait_send()
-    kv_down.wait_send()
-    kv_up.wait_send()
+    kv_pieces(lambda c: c.wait_send())
     whole(snd1, rcv1, a1_s, a1_r).wait_send()
     whole(snd2, rcv2, a2_s, a2_r).wait_send()
     for e in (8, 9, 10, 1, 2, 3):
@@ -440,8 +453,8 @@
             dma((4,)),
             dma((4,)),
             dma((4,)),
-            dma((2,)),
-            dma((2,)),
+            dma((2, 3, 4)),
+            dma((2, 3, 4)),
             dma((4,)),
             dma((4,)),
             dma((4,)),

time: 53.9 us -> 59.7 us (1.11)
  Pallas kernels: 53.1 us -> 58.7 us
    pallas_call x1, Pallas kernels: 51.9 us -> 57.5 us  [body(): pl.pallas_call(kernel, out_shape=(vm((ROWS, WIDE), BF), vm((KV, D, WIDE),...]
where the time goes in v9:
time: 59.7 us; the launch traced here: 59.4 us
  Pallas kernels  58.7 us (98%)
  between operations  0.64 us (1%)
    pallas_call x1, Pallas kernels, body(): pl.pallas_call(kernel, out_shape=(vm((ROWS, WIDE), BF), vm((KV, D, WIDE),...  57.5 us
    pallas_call x1, Pallas kernels, body(): pl.pallas_call(finish, out_shape=(jax.ShapeDtypeStruct((D, KV * WIDE), BF...  1.24 us

profile of v9, /device:TPU:2, one launch (start us, length us, event | category | flops | bytes accessed | tf_op | source)
XLA Modules:
  0.0 59.4 jit_solution(10511756946046044620)
XLA Ops:
  0.6 57.5 %shard_map.102 = (bf16[512,640]{1,0:T(8,128)(2,1)S(1)}, bf16[4,128,640]{2,1,0:T(8,128)(2,1)S(1)}, bf16[4,128,256]{2,1,0:T(8,128)(2,1)S(1)}, bf16[4,128,256]{2,1,...) custom-call(bf16[128,2560]{1,0:T(8,128)(2,1)} %q_hbm.1, bf16[128,512]{1,0:T(8,128)(2,1)} %k_hbm.1, ...), custom_call_target="tpu_custom_call" | custom-call | tf_op jit(solution)/shard_map/pallas_call | solution.py:413
  58.1 1.2 %shard_map.103 = (bf16[128,2560]{1,0:T(8,128)(2,1)}, bf16[128,2560]{1,0:T(8,128)(2,1)}, bf16[128,512]{1,0:T(8,128)(2,1)}, bf16[128,512]{1,0:T(8,128)(2,1)}) custom-call(bf16[512,640]{1,0:T(8,128)(2,1)S(1)} %get-tuple-element.10.got, bf16[4,128,640]{2,1,0:T(8,128)(2,1)S(1)} %get-tuple-element.11.qg, bf16[4,128,256]{2,1,0:T(8,128)(2,1)S(1)} %get-tuple-element.12.grow, ...), custom_call_target="tpu_custom_call" | custom-call | tf_op jit(solution)/shard_map/pallas_call | solution.py:473

commit v10 on v9

--- a/solution.py
+++ b/solution.py
@@ -62,7 +62,7 @@
     rcv2, qg, grow, gup, gdn, p_out,
     sizes, ffn_ref, att_ref, qb, kvb, qst, kvw, kall, prob, gin, snd1, rcv1, snd2,
     m_att, mt_att, ott, dos, sc, dsb, dqs, accw, gsend, bias, invs, flag,
-    in_sem, att_s, att_r, kv_s, kv_r, kz_s, kz_r, q_s, q_r, dq_s, dq_r, g_s, g_r,
+    in_sem, att_s, att_r, kv_s, kv_r, kz_s, kz_r, f_s, f_r, q_s, q_r, dq_s, dq_r, g_s, g_r,
     a1_s, a1_r, a2_s, a2_r,
 ):
     dp = lax.axis_index("dp")
@@ -170,6 +170,13 @@
         g = (x + i) & 3
         return remote(qb.at[g], qst.at[x], q_s.at[i], q_r.at[x], z * KV + g)
 
+    QUARTER = D // 4
+
+    def far_copy(k):
+        rows = slice(k * QUARTER, (k + 1) * QUARTER)
+        g = x ^ 2
+        return remote(qb.at[g, rows], qst.at[x, rows], f_s.at[k], f_r.at[k], z * KV + g)
+
     for i in (1, 3):
         q_copy(i).start()
 
@@ -190,8 +197,7 @@
     def send1(dx):
         send_column(snd1, rcv1, token_row, rows_at, a1_s, a1_r, dx)
 
-    for dx in (0, 1, 3, 2):
-        send1(dx)
+    send1(0)
     rcv1[rows_at(me), :] = snd1[token_row(me), :]
 
     def whole(src, dst, s, r):
@@ -219,7 +225,13 @@
     for i in (1, 3, 2):
         kv_arrived(i)
     kv_pieces(lambda c: c.start())
-    q_copy(2).start()
+    for k in range(4):
+        far_copy(k).start()
+    for i in (1, 3):
+        u = (x + i) & 3
+        remote(qb.at[0], qst.at[u], q_s.at[0], q_r.at[u], me ^ 1).wait_recv()
+    for dx in (1, 3, 2):
+        send1(dx)
     accw[...] = jnp.zeros_like(accw)
     invs[...] = jnp.zeros_like(invs)
 
@@ -236,9 +248,10 @@
     def forward(i, _):
         u = (x + (0xB4 >> (2 * i))) & 3
 
-        @pl.when(i > 0)
+        @pl.when(i == 3)
         def _():
-            remote(qb.at[0], qst.at[u], q_s.at[0], q_r.at[u], me ^ 1).wait_recv()
+            for k in range(4):
+                far_copy(k).wait_recv()
 
         kall[u, 0:D, :] = kvw[4 + u]
         for r in (1, 2, 3):
@@ -358,7 +371,10 @@
     for i in (1, 2, 3):
         order_copy(i).wait_send()
         kv_copy(i).wait_send()
+    for i in (1, 3):
         q_copy(i).wait_send()
+    for k in range(4):
+        far_copy(k).wait_send()
     kv_pieces(lambda c: c.wait_send())
     whole(snd1, rcv1, a1_s, a1_r).wait_send()
     whole(snd2, rcv2, a2_s, a2_r).wait_send()
@@ -459,6 +475,8 @@
             dma((4,)),
             dma((4,)),
             dma((4,)),
+            dma((4,)),
+            dma((4,)),
             dma((12,)),
             dma((3, 4)),
             dma,

time: 59.7 us -> 55.7 us (0.933)
  Pallas kernels: 58.7 us -> 54.9 us
    pallas_call x1, Pallas kernels: 57.5 us -> 53.7 us  [body(): pl.pallas_call(kernel, out_shape=(vm((ROWS, WIDE), BF), vm((KV, D, WIDE),...]
where the time goes in v10:
time: 55.7 us; the launch traced here: 55.6 us
  Pallas kernels  54.9 us (99%)
  between operations  0.64 us (1%)
    pallas_call x1, Pallas kernels, body(): pl.pallas_call(kernel, out_shape=(vm((ROWS, WIDE), BF), vm((KV, D, WIDE),...  53.7 us
    pallas_call x1, Pallas kernels, body(): pl.pallas_call(finish, out_shape=(jax.ShapeDtypeStruct((D, KV * WIDE), BF...  1.24 us

profile of v10, /device:TPU:2, one launch (start us, length us, event | category | flops | bytes accessed | tf_op | source)
XLA Modules:
  0.0 55.6 jit_solution(81486556201707983)
XLA Ops:
  0.6 53.7 %shard_map.102 = (bf16[512,640]{1,0:T(8,128)(2,1)S(1)}, bf16[4,128,640]{2,1,0:T(8,128)(2,1)S(1)}, bf16[4,128,256]{2,1,0:T(8,128)(2,1)S(1)}, bf16[4,128,256]{2,1,...) custom-call(bf16[128,2560]{1,0:T(8,128)(2,1)} %q_hbm.1, bf16[128,512]{1,0:T(8,128)(2,1)} %k_hbm.1, ...), custom_call_target="tpu_custom_call" | custom-call | tf_op jit(solution)/shard_map/pallas_call | solution.py:429
  54.3 1.2 %shard_map.103 = (bf16[128,2560]{1,0:T(8,128)(2,1)}, bf16[128,2560]{1,0:T(8,128)(2,1)}, bf16[128,512]{1,0:T(8,128)(2,1)}, bf16[128,512]{1,0:T(8,128)(2,1)}) custom-call(bf16[512,640]{1,0:T(8,128)(2,1)S(1)} %get-tuple-element.10.got, bf16[4,128,640]{2,1,0:T(8,128)(2,1)S(1)} %get-tuple-element.11.qg, bf16[4,128,256]{2,1,0:T(8,128)(2,1)S(1)} %get-tuple-element.12.grow, ...), custom_call_target="tpu_custom_call" | custom-call | tf_op jit(solution)/shard_map/pallas_call | solution.py:491

commit v11 on v5

--- a/solution.py
+++ b/solution.py
@@ -108,6 +108,44 @@
     for c in local[4:] + local[:4]:
         c.start()
 
+    for c in local[2:]:
+        c.wait()
+    kvw[4 + x] = kvb[x]
+    qst[x] = qb[x]
+
+    pl.semaphore_wait(barrier, N - 1)
+
+    def order_copy(i):
+        return remote(att_ref.at[x], att_ref.at[x], att_s.at[i], att_r.at[i], z * KV + ((x + i) & 3))
+
+    def order_arrived(i):
+        u = (x + 4 - i) & 3
+        return remote(att_ref.at[u], att_ref.at[u], att_s.at[i], att_r.at[i], me ^ 1)
+
+    for i in (1, 2, 3):
+        order_copy(i).start()
+
+    def kv_copy(i):
+        g = (x + i) & 3
+        return remote(kvb.at[g], kvw.at[4 + x], kv_s.at[i], kv_r.at[x], z * KV + g)
+
+    def kv_arrived(i):
+        u = (x + i) & 3
+        remote(kvb.at[u], kvw.at[4 + u], kv_s.at[i], kv_r.at[u], z * KV + u).wait_recv()
+
+    kv_down = remote(kvw.at[4:7], kvw.at[8:11], kz_s.at[0], kz_r.at[0], below + x)
+    kv_up = remote(kvw.at[5:8, 0:HALF], kvw.at[1:4, 0:HALF], kz_s.at[1], kz_r.at[1], above + x)
+
+    for i in (2, 1, 3):
+        kv_copy(i).start()
+
+    def q_copy(i):
+        g = (x + i) & 3
+        return remote(qb.at[g], qst.at[x], q_s.at[i], q_r.at[x], z * KV + g)
+
+    for i in (1, 3):
+        q_copy(i).start()
+
     local[0].wait()
     order = ffn_ref[...].astype(F32)
     p_ffn = (order == iota((D, D), 0).astype(F32)).astype(BF)
@@ -117,44 +155,6 @@
     packed = dot(gather_ffn, gin[...], 1, 0).astype(BF)
     for g in range(KV):
         snd1[g * D : (g + 1) * D, :] = packed[:, g * WIDE : (g + 1) * WIDE]
-
-    for c in local[2:]:
-        c.wait()
-    kvw[4 + x] = kvb[x]
-    qst[x] = qb[x]
-
-    pl.semaphore_wait(barrier, N - 1)
-
-    def order_copy(i):
-        return remote(att_ref.at[x], att_ref.at[x], att_s.at[i], att_r.at[i], z * KV + ((x + i) & 3))
-
-    def order_arrived(i):
-        u = (x + 4 - i) & 3
-        return remote(att_ref.at[u], att_ref.at[u], att_s.at[i], att_r.at[i], me ^ 1)
-
-    for i in (1, 2, 3):
-        order_copy(i).start()
-
-    def kv_copy(i):
-        g = (x + i) & 3
-        return remote(kvb.at[g], kvw.at[4 + x], kv_s.at[i], kv_r.at[x], z * KV + g)
-
-    def kv_arrived(i):
-        u = (x + i) & 3
-        remote(kvb.at[u], kvw.at[4 + u], kv_s.at[i], kv_r.at[u], z * KV + u).wait_recv()
-
-    kv_down = remote(kvw.at[4:7], kvw.at[8:11], kz_s.at[0], kz_r.at[0], below + x)
-    kv_up = remote(kvw.at[5:8, 0:HALF], kvw.at[1:4, 0:HALF], kz_s.at[1], kz_r.at[1], above + x)
-
-    for i in (2, 1, 3):
-        kv_copy(i).start()
-
-    def q_copy(i):
-        g = (x + i) & 3
-        return remote(qb.at[g], qst.at[x], q_s.at[i], q_r.at[x], z * KV + g)
-
-    for i in (1, 3):
-        q_copy(i).start()
 
     def rows_at(i):
         return pl.ds(pl.multiple_of(i * CHUNK, CHUNK), CHUNK)

time: 53.9 us -> 53.9 us (level)
  no operation moved by 1% of the time
where the time goes in v11:
time: 53.9 us; the launch traced here: 53.8 us
  Pallas kernels  53.1 us (99%)
  between operations  0.64 us (1%)
    pallas_call x1, Pallas kernels, body(): pl.pallas_call(kernel, out_shape=(vm((ROWS, WIDE), BF), vm((KV, D, WIDE),...  51.9 us
    pallas_call x1, Pallas kernels, body(): pl.pallas_call(finish, out_shape=(jax.ShapeDtypeStruct((D, KV * WIDE), BF...  1.24 us

profile of v11, /device:TPU:2, one launch (start us, length us, event | category | flops | bytes accessed | tf_op | source)
XLA Modules:
  0.0 53.8 jit_solution(2255877545590148725)
XLA Ops:
  0.6 51.9 %shard_map.102 = (bf16[512,640]{1,0:T(8,128)(2,1)S(1)}, bf16[4,128,640]{2,1,0:T(8,128)(2,1)S(1)}, bf16[4,128,256]{2,1,0:T(8,128)(2,1)S(1)}, bf16[4,128,256]{2,1,...) custom-call(bf16[128,2560]{1,0:T(8,128)(2,1)} %q_hbm.1, bf16[128,512]{1,0:T(8,128)(2,1)} %k_hbm.1, ...), custom_call_target="tpu_custom_call" | custom-call | tf_op jit(solution)/shard_map/pallas_call | solution.py:400
  52.5 1.2 %shard_map.103 = (bf16[128,2560]{1,0:T(8,128)(2,1)}, bf16[128,2560]{1,0:T(8,128)(2,1)}, bf16[128,512]{1,0:T(8,128)(2,1)}, bf16[128,512]{1,0:T(8,128)(2,1)}) custom-call(bf16[512,640]{1,0:T(8,128)(2,1)S(1)} %get-tuple-element.10.got, bf16[4,128,640]{2,1,0:T(8,128)(2,1)S(1)} %get-tuple-element.11.qg, bf16[4,128,256]{2,1,0:T(8,128)(2,1)S(1)} %get-tuple-element.12.grow, ...), custom_call_target="tpu_custom_call" | custom-call | tf_op jit(solution)/shard_map/pallas_call | solution.py:460

commit v12 on v5

--- a/solution.py
+++ b/solution.py
@@ -59,10 +59,10 @@
 
 def kernel(
     q_hbm, k_hbm, v_hbm, g_hbm, sizes_hbm, ffn_hbm, att_hbm,
-    rcv2, qg, grow, gup, gdn, p_out,
+    rcv2, qg, grow, p_out,
     sizes, ffn_ref, att_ref, qb, kvb, qst, kvw, kall, prob, gin, snd1, rcv1, snd2,
-    m_att, mt_att, ott, dos, sc, dsb, dqs, accw, gsend, bias, invs, flag,
-    in_sem, att_s, att_r, kv_s, kv_r, kz_s, kz_r, q_s, q_r, dq_s, dq_r, g_s, g_r,
+    m_att, mt_att, ott, dos, sc, dsb, dqs, accw, gsend, gup, gdn, bias, invs, flag,
+    in_sem, att_s, att_r, kv_s, kv_r, kz_s, kz_r, q_s, q_r, dq_s, dq_r, g_s, g_r, gz_s, gz_r,
     a1_s, a1_r, a2_s, a2_r,
 ):
     dp = lax.axis_index("dp")
@@ -314,32 +314,39 @@
     lax.fori_loop(0, KV, backward, 0)
     qg[x] = dqs[x]
 
-    for e in range(1, 11):
+    for e in (8, 9, 10, 1, 2, 3):
         gsend[e] = accw[e].astype(BF)
-
-    def g_copy(e):
-        g = e & 3
-        if e < 4:
-            return remote(gsend.at[e, 0:HALF], gdn.at[x], g_s.at[e], g_r.at[0, x], below + g)
-        if e < 8:
-            return remote(gsend.at[e], grow.at[x], g_s.at[e], g_r.at[1, x], z * KV + g)
-        return remote(gsend.at[e], gup.at[x], g_s.at[e], g_r.at[2, x], above + g)
-
-    for e in (8, 9, 10, 1, 2, 3):
-        g_copy(e).start()
-    for e in range(4, 8):
-        pl.when(x != e - 4)(g_copy(e).start)
+    g_up = remote(gsend.at[8:11], gup, gz_s.at[0], gz_r.at[0], above + x)
+    g_down = remote(gsend.at[1:4, 0:HALF], gdn, gz_s.at[1], gz_r.at[1], below + x)
+    g_up.start()
+    g_down.start()
+    g_up.wait_recv()
+    g_down.wait_recv()
+    for u in range(KV):
+        total = accw[4 + u]
+        if u < 3:
+            total = total + gup[u].astype(F32)
+        low = total[0:HALF]
+        if u > 0:
+            low = low + gdn[u - 1].astype(F32)
+        gsend[4 + u, 0:HALF, :] = low.astype(BF)
+        gsend[4 + u, HALF:D, :] = total[HALF:D].astype(BF)
+
+    def g_copy(i):
+        u = (x + i) & 3
+        return remote(gsend.at[4 + u], grow.at[x], g_s.at[i], g_r.at[x], z * KV + u)
+
+    for i in (2, 1, 3):
+        g_copy(i).start()
     grow[x] = gsend[4 + x]
 
     whole(snd2, rcv2, a2_s, a2_r).wait_recv()
-    for g in range(KV):
-        pl.when(x != g)(
-            remote(gsend.at[4], grow.at[g], g_s.at[0], g_r.at[1, g], me ^ 1).wait_recv
-        )
-        pl.when(x <= 2)(remote(gsend.at[4], gup.at[g], g_s.at[0], g_r.at[2, g], me ^ 1).wait_recv)
-        pl.when(x >= 1)(
-            remote(gsend.at[4, 0:HALF], gdn.at[g], g_s.at[0], g_r.at[0, g], me ^ 1).wait_recv
-        )
+    for i in (1, 2, 3):
+        u = (x + i) & 3
+        remote(gsend.at[4], grow.at[u], g_s.at[i], g_r.at[u], me ^ 1).wait_recv()
+        g_copy(i).wait_send()
+    g_up.wait_send()
+    g_down.wait_send()
 
     for i in (1, 2, 3):
         order_copy(i).wait_send()
@@ -349,23 +356,19 @@
     kv_up.wait_send()
     whole(snd1, rcv1, a1_s, a1_r).wait_send()
     whole(snd2, rcv2, a2_s, a2_r).wait_send()
-    for e in (8, 9, 10, 1, 2, 3):
-        g_copy(e).wait_send()
     for u in range(KV):
 
         @pl.when(x != u)
         def _():
-            g_copy(4 + u).wait_send()
             dq_copy(u).wait_send()
             remote(dqs.at[u], qg.at[u], dq_s.at[u], dq_r.at[u], me ^ 1).wait_recv()
 
 
 def finish(
-    got, qg, grow, gup, gdn, p_ffn,
+    got, qg, grow, p_ffn,
     out_hbm, qg_hbm, kg_hbm, vg_hbm,
-    out_v, kg_v, vg_v, sem,
+    out_v, sem,
 ):
-    x = lax.axis_index("ctx") & 3
     outs = []
 
     def send(src, dst):
@@ -374,19 +377,12 @@
 
     for g in range(KV):
         send(qg.at[g], qg_hbm.at[:, g * WIDE : (g + 1) * WIDE])
-    for g in range(KV):
-        total = grow[g].astype(F32) + jnp.where(x <= 2, gup[g].astype(F32), 0.0)
-        low = total[0:HALF] + jnp.where(x >= 1, gdn[g].astype(F32), 0.0)
-        high = total[HALF:D]
-        cols = slice(g * D, (g + 1) * D)
-        for ref, lane in ((kg_v, 0), (vg_v, D)):
-            ref[0:HALF, cols] = low[:, lane : lane + D].astype(BF)
-            ref[HALF:D, cols] = high[:, lane : lane + D].astype(BF)
-    send(kg_v, kg_hbm)
-    send(vg_v, vg_hbm)
+        send(grow.at[g, :, 0:D], kg_hbm.at[:, g * D : (g + 1) * D])
+        send(grow.at[g, :, D:], vg_hbm.at[:, g * D : (g + 1) * D])
     for g in range(KV):
         cols = slice(g * WIDE, (g + 1) * WIDE)
-        out_v[:, cols] = dot(p_ffn[...], got[g * D : (g + 1) * D, :], 1, 0).astype(BF)
+        rows = got[g * D : (g + 1) * D, :]
+        out_v[:, cols] = dot(p_ffn[...], rows, 1, 0).astype(BF)
         send(out_v.at[:, cols], out_hbm.at[:, cols])
     for c in outs:
         c.wait()
@@ -397,18 +393,16 @@
     vmem = pl.BlockSpec(memory_space=pltpu.VMEM)
     dma = pltpu.SemaphoreType.DMA
     vm = pltpu.VMEM
-    got, qg, row, up, down, p_ffn = pl.pallas_call(
+    got, qg, row, p_ffn = pl.pallas_call(
         kernel,
         out_shape=(
             vm((ROWS, WIDE), BF),
             vm((KV, D, WIDE), BF),
             vm((KV, D, 2 * D), BF),
-            vm((KV, D, 2 * D), BF),
-            vm((KV, HALF, 2 * D), BF),
             vm((D, D), BF),
         ),
         in_specs=[hbm] * 7,
-        out_specs=(vmem,) * 6,
+        out_specs=(vmem,) * 4,
         scratch_shapes=[
             pltpu.SMEM((16,), jnp.int32),
             vm((1, D), jnp.int32),
@@ -432,6 +426,8 @@
             vm((KV, D, WIDE), BF),
             vm((12, D, 2 * D), F32),
             vm((12, D, 2 * D), BF),
+            vm((3, D, 2 * D), BF),
+            vm((3, HALF, 2 * D), BF),
             vm((KV, KEYS, D), F32),
             vm((KV, 8, D), F32),
             pltpu.SMEM((KV * KV,), jnp.int32),
@@ -446,8 +442,10 @@
             dma((4,)),
             dma((4,)),
             dma((4,)),
-            dma((12,)),
-            dma((3, 4)),
+            dma((4,)),
+            dma((4,)),
+            dma((2,)),
+            dma((2,)),
             dma,
             dma,
             dma,
@@ -465,16 +463,14 @@
             jax.ShapeDtypeStruct((D, KV * D), BF),
             jax.ShapeDtypeStruct((D, KV * D), BF),
         ),
-        in_specs=[vmem] * 6,
+        in_specs=[vmem] * 4,
         out_specs=(hbm,) * 4,
         scratch_shapes=[
             vm((D, KV * WIDE), BF),
-            vm((D, KV * D), BF),
-            vm((D, KV * D), BF),
-            dma((10,)),
+            dma((16,)),
         ],
         compiler_params=pltpu.CompilerParams(vmem_limit_bytes=8 * 1024 * 1024),
-    )(got, qg, row, up, down, p_ffn)
+    )(got, qg, row, p_ffn)
 
 
 def solution(mesh):

time: 53.9 us -> 56.4 us (1.046)
  the two profiles are of different devices: /device:TPU:2 before, /device:TPU:8 now
where the time goes in v12:
time: 56.4 us; the launch traced here: 56.3 us
  Pallas kernels  55.7 us (99%)
  between operations  0.64 us (1%)
    pallas_call x1, Pallas kernels, body(): pl.pallas_call(kernel, out_shape=(vm((ROWS, WIDE), BF), vm((KV, D, WIDE),...  54.4 us
    pallas_call x1, Pallas kernels, body(): pl.pallas_call(finish, out_shape=(jax.ShapeDtypeStruct((D, KV * WIDE), BF...  1.29 us

profile of v12, /device:TPU:8, one launch (start us, length us, event | category | flops | bytes accessed | tf_op | source)
XLA Modules:
  0.0 56.3 jit_solution(7071345914862854744)
XLA Ops:
  0.6 54.4 %shard_map.102 = (bf16[512,640]{1,0:T(8,128)(2,1)S(1)}, bf16[4,128,640]{2,1,0:T(8,128)(2,1)S(1)}, bf16[4,128,256]{2,1,0:T(8,128)(2,1)S(1)}, bf16[128,128]{1,0:T(8,128)(2,1)S(1)}) custom-call(bf16[128,2560]{1,0:T(8,128)(2,1)} %q_hbm.1, bf16[128,512]{1,0:T(8,128)(2,1)} %k_hbm.1, bf16[128,512]{1,0:T(8,128)(2,1)} %v_hbm.1, bf16[128,2560]{1,0:T(8,128)(2,1)} %g_hbm.1, ...), custom_call_target="tpu_custom_call" | custom-call | tf_op jit(solution)/shard_map/pallas_call | solution.py:396
  55.0 1.3 %shard_map.103 = (bf16[128,2560]{1,0:T(8,128)(2,1)}, bf16[128,2560]{1,0:T(8,128)(2,1)}, bf16[128,512]{1,0:T(8,128)(2,1)}, bf16[128,512]{1,0:T(8,128)(2,1)}) custom-call(bf16[512,640]{1,0:T(8,128)(2,1)S(1)} %get-tuple-element.8.got, bf16[4,128,640]{2,1,0:T(8,128)(2,1)S(1)} %get-tuple-element.9.qg, bf16[4,128,256]{2,1,0:T(8,128)(2,1)S(1)} %get-tuple-element.10.grow, ...), custom_call_target="tpu_custom_call" | custom-call | tf_op jit(solution)/shard_map/pallas_call | solution.py:458

commit v13 on v6

--- a/solution.py
+++ b/solution.py
@@ -62,7 +62,7 @@
     rcv2, qg, grow, gup, gdn, p_out,
     sizes, ffn_ref, att_ref, qb, kvb, qst, kvw, kall, prob, gin, snd1, rcv1, snd2,
     m_att, mt_att, ott, dos, sc, dsb, dqs, accw, gsend, bias, invs, flag,
-    in_sem, att_s, att_r, kv_s, kv_r, kz_s, kz_r, f_s, f_r, q_s, q_r, dq_s, dq_r, g_s, g_r,
+    in_sem, att_s, att_r, kv_s, kv_r, kz_s, kz_r, q_s, q_r, dq_s, dq_r, g_s, g_r,
     a1_s, a1_r, a2_s, a2_r,
 ):
     dp = lax.axis_index("dp")
@@ -142,13 +142,6 @@
     def q_copy(i):
         g = (x + i) & 3
         return remote(qb.at[g], qst.at[x], q_s.at[i], q_r.at[x], z * KV + g)
-
-    QUARTER = D // 4
-
-    def far_copy(k):
-        rows = slice(k * QUARTER, (k + 1) * QUARTER)
-        g = x ^ 2
-        return remote(qb.at[g, rows], qst.at[x, rows], f_s.at[k], f_r.at[k], z * KV + g)
 
     for i in (1, 3):
         q_copy(i).start()
@@ -209,8 +202,7 @@
         kv_arrived(i)
     kv_down.start()
     kv_up.start()
-    for k in range(4):
-        far_copy(k).start()
+    q_copy(2).start()
     for dx in (1, 3, 2):
         send1(dx)
     accw[...] = jnp.zeros_like(accw)
@@ -230,14 +222,9 @@
     def forward(i, _):
         u = (x + (0xB4 >> (2 * i))) & 3
 
-        @pl.when((i == 1) | (i == 2))
+        @pl.when(i > 0)
         def _():
             remote(qb.at[0], qst.at[u], q_s.at[0], q_r.at[u], me ^ 1).wait_recv()
-
-        @pl.when(i == 3)
-        def _():
-            for k in range(4):
-                far_copy(k).wait_recv()
 
         kall[u, 0:D, :] = kvw[4 + u]
         for r in (1, 2, 3):
@@ -381,10 +368,7 @@
     for i in (1, 2, 3):
         order_copy(i).wait_send()
         kv_copy(i).wait_send()
-    for i in (1, 3):
         q_copy(i).wait_send()
-    for k in range(4):
-        far_copy(k).wait_send()
     kv_down.wait_send()
     kv_up.wait_send()
     whole(snd1, rcv1, a1_s, a1_r).wait_send()
@@ -484,8 +468,6 @@
             dma((4,)),
             dma((4,)),
             dma((4,)),
-            dma((4,)),
-            dma((4,)),
             dma((2, 12)),
             dma((3, 2, 4)),
             dma,

time: 54.3 us -> 54.3 us (level)
  no operation moved by 1% of the time
where the time goes in v13:
time: 54.3 us; the launch traced here: 54.1 us
  Pallas kernels  53.5 us (99%)
  between operations  0.64 us (1%)
    pallas_call x1, Pallas kernels, body(): pl.pallas_call(kernel, out_shape=(vm((ROWS, WIDE), BF), vm((KV, D, WIDE),...  52.3 us
    pallas_call x1, Pallas kernels, body(): pl.pallas_call(finish, out_shape=(jax.ShapeDtypeStruct((D, KV * WIDE), BF...  1.24 us

profile of v13, /device:TPU:2, one launch (start us, length us, event | category | flops | bytes accessed | tf_op | source)
XLA Modules:
  0.0 54.1 jit_solution(4964581667242920539)
XLA Ops:
  0.6 52.3 %shard_map.102 = (bf16[512,640]{1,0:T(8,128)(2,1)S(1)}, bf16[4,128,640]{2,1,0:T(8,128)(2,1)S(1)}, bf16[4,2,128,128]{3,2,1,0:T(8,128)(2,1)S(1)}, bf16[4,2,128,128...) custom-call(bf16[128,2560]{1,0:T(8,128)(2,1)} %q_hbm.1, ...), custom_call_target="tpu_custom_call" | custom-call | tf_op jit(solution)/shard_map/pallas_call | solution.py:422
  52.9 1.2 %shard_map.103 = (bf16[128,2560]{1,0:T(8,128)(2,1)}, bf16[128,2560]{1,0:T(8,128)(2,1)}, bf16[128,512]{1,0:T(8,128)(2,1)}, bf16[128,512]{1,0:T(8,128)(2,1)}) custom-call(bf16[512,640]{1,0:T(8,128)(2,1)S(1)} %get-tuple-element.10.got, bf16[4,128,640]{2,1,0:T(8,128)(2,1)S(1)} %get-tuple-element.11.qg, bf16[4,2,128,128]{3,2,1,0:T(8,128)(2,1)S(1)} %get-tuple-element.12.grow, ...), custom_call_target="tpu_custom_call" | custom-call | tf_op jit(solution)/shard_map/pallas_call | solution.py:482

commit v14 on v5

--- a/solution.py
+++ b/solution.py
@@ -292,10 +292,10 @@
 
         for rows in blocks:
             dsb[rows, :] = (prob[u, rows, :].astype(F32) * (sc[rows, :] - delta)).astype(BF)
-        dq = dot(keys.T, dsb[...], 1, 0) * scale
+        dq = (dot(keys.T, dsb[...], 1, 0) * scale).astype(BF)
         for a in range(GR):
             cols = slice(a * D, (a + 1) * D)
-            dqs[u, :, cols] = dq[:, cols].T.astype(BF)
+            dqs[u, :, cols] = dq[:, cols].T
 
         @pl.when(i < 3)
         def _():

time: 53.9 us -> 53.8 us (level)
  no operation moved by 1% of the time
where the time goes in v14:
time: 53.8 us; the launch traced here: 53.7 us
  Pallas kernels  53.1 us (99%)
  between operations  0.64 us (1%)
    pallas_call x1, Pallas kernels, body(): pl.pallas_call(kernel, out_shape=(vm((ROWS, WIDE), BF), vm((KV, D, WIDE),...  51.8 us
    pallas_call x1, Pallas kernels, body(): pl.pallas_call(finish, out_shape=(jax.ShapeDtypeStruct((D, KV * WIDE), BF...  1.24 us

profile of v14, /device:TPU:2, one launch (start us, length us, event | category | flops | bytes accessed | tf_op | source)
XLA Modules:
  0.0 53.7 jit_solution(4266191975097545186)
XLA Ops:
  0.6 51.8 %shard_map.102 = (bf16[512,640]{1,0:T(8,128)(2,1)S(1)}, bf16[4,128,640]{2,1,0:T(8,128)(2,1)S(1)}, bf16[4,128,256]{2,1,0:T(8,128)(2,1)S(1)}, bf16[4,128,256]{2,1,...) custom-call(bf16[128,2560]{1,0:T(8,128)(2,1)} %q_hbm.1, bf16[128,512]{1,0:T(8,128)(2,1)} %k_hbm.1, ...), custom_call_target="tpu_custom_call" | custom-call | tf_op jit(solution)/shard_map/pallas_call | solution.py:400
  52.5 1.2 %shard_map.103 = (bf16[128,2560]{1,0:T(8,128)(2,1)}, bf16[128,2560]{1,0:T(8,128)(2,1)}, bf16[128,512]{1,0:T(8,128)(2,1)}, bf16[128,512]{1,0:T(8,128)(2,1)}) custom-call(bf16[512,640]{1,0:T(8,128)(2,1)S(1)} %get-tuple-element.10.got, bf16[4,128,640]{2,1,0:T(8,128)(2,1)S(1)} %get-tuple-element.11.qg, bf16[4,128,256]{2,1,0:T(8,128)(2,1)S(1)} %get-tuple-element.12.grow, ...), custom_call_target="tpu_custom_call" | custom-call | tf_op jit(solution)/shard_map/pallas_call | solution.py:460
